TPU v7x, 32 devices: a whole 2x2x4 slice. The times are simulated.
32 devices in a mesh: tm: 4 (over y, core), space: 8 (over z, x).
Axes of the slice: x: 2, y: 2, z: 4, core: 2. Of those that a mesh axis runs over, the one named last changes fastest.
Arguments:
- slab_states: float32 [4, 2, 64, 32, 512], P('tm', None, 'space'), may hold values from -6 to 6
- velocity: float32 [2, 3, 64, 32, 512], P(None, None, 'space'), may hold values from -0.9 to 0.9
- snap_of_step: int32 [4, 2], P('tm'), may hold values from 0 to 1
Outputs:
- slab_starts: float32 [4, 2, 64, 32, 512], P('tm', None, 'space')
- heater_grad: float32 [64, 32, 512], P('space', 'tm')
All inputs are finite; a program needn't handle non-finite values.
Results may differ from a plain program's by a relative error of at most 0.00002.
Values sent between devices are 32-bit elements; how exact they have to be, the bound alone decides.
A program may use at most 64 MiB of HBM per device.

v0:
```python
import jax
import jax.numpy as jnp
from jax import lax
from jax.sharding import PartitionSpec as P

coupling = 0.3


def with_halo(array, sides, width):
    for axis, dim in sides:
        devices, length = (lax.axis_size(axis), array.shape[dim])
        up = [(i, (i + 1) % devices) for i in range(devices - 1)]
        down = [(j, i) for i, j in up]
        last = lax.slice_in_dim(array, length - width, length, axis=dim)
        first = lax.slice_in_dim(array, 0, width, axis=dim)
        before = lax.ppermute(last, axis, up)
        after = lax.ppermute(first, axis, down)
        array = jnp.concatenate([before, array, after], axis=dim)
    return array


def passed_along(array, axis, by):
    devices = lax.axis_size(axis)
    pairs = [(i, i + by) for i in range(devices) if 0 <= i + by < devices]
    return lax.ppermute(array, axis, pairs)


def advance(widened, flow):
    centre = widened[:, 1:-1]
    east_side = widened[:, 2:]
    west_side = widened[:, :-2]
    north_side = jnp.pad(centre, ((0, 0), (0, 0), (0, 1), (0, 0)))[:, :, 1:]
    south_side = jnp.pad(centre, ((0, 0), (0, 0), (1, 0), (0, 0)))[:, :, :-1]
    upper_side = jnp.pad(centre, ((0, 0), (0, 0), (0, 0), (0, 1)))[:, :, :, 1:]
    lower_side = jnp.pad(centre, ((0, 0), (0, 0), (0, 0), (1, 0)))[:, :, :, :-1]
    laplace = (
        east_side + west_side + north_side + south_side + upper_side + lower_side - 6.0 * centre
    )
    transport = (
        flow[0] * (east_side - west_side)
        + flow[1] * (north_side - south_side)
        + flow[2] * (upper_side - lower_side)
    )
    temper = centre[0] + 0.14 * laplace[0] + 0.25 * transport[0] + coupling * centre[1]
    dopant = centre[1] + 0.06 * laplace[1] + 0.25 * transport[1]
    return jnp.stack([temper, dopant])


def sweep_local(adjoint, flow_bank, snaps, keep_total):
    steps_count = snaps.shape[0]
    total = jnp.zeros(adjoint.shape[1:], jnp.float32)
    for step_index in reversed(range(steps_count)):
        flow = lax.dynamic_index_in_dim(flow_bank, snaps[step_index], 0, keepdims=False)
        widened = with_halo(adjoint, (("space", 1),), 1)
        adjoint = advance(widened, flow)
        if keep_total:
            total = total + adjoint[0]
    return (adjoint, total)


def body(slab_states, velocity, snap_of_step):
    start = slab_states[0]
    snaps = snap_of_step[0]
    first, unused = sweep_local(start, velocity, snaps, False)
    received = passed_along(first, "tm", -1)
    is_last = lax.axis_index("tm") == lax.axis_size("tm") - 1
    carried = jnp.where(is_last, start, received)
    final, total = sweep_local(carried, velocity, snaps, True)
    gradient = lax.psum_scatter(total, "tm", scatter_dimension=1, tiled=True) / snaps.shape[0]
    return (final[None], gradient)


def solution(mesh):
    placed = (P("tm", None, "space", None, None), P(None, None, "space", None, None), P("tm", None))
    return jax.shard_map(
        body,
        mesh=mesh,
        in_specs=placed,
        out_specs=(P("tm", None, "space", None, None), P("space", "tm", None)),
        check_vma=False,
    )
```

profile of v0, /device:TPU:0, one launch (start us, length us, event | category | flops | bytes accessed | tf_op | source)
XLA Modules:
  0.0 112.7 jit_solution(5677259374424687414)
XLA Ops:
  7.2 0.0 reduce-scatter.2.cloned.1.call-start
  7.2 1.0 fusion.23
  8.2 1.3 %collective-permute-start = (f32[2,1,32,512]{3,2,1,0:T(8,128)S(1)}, f32[2,1,32,512]{3,2,1,0:T(8,128)S(1)}, u32[]{:S(2)}, u32[]{:S(2)}) collective-permute-start(f32[2,1,32,512]{3,2,1,0:T(8,128)S(1)} %get-tuple-element.23), channel_id=1, source_target_pairs={{1,0},{2,1},{3,2},{4,3},{5,4},{6,5},{7,6},{9,8},{10,9},{11,10},{12... | collective-permute-start | bytes 393224 | tf_op jit(solution)/shard_map/ppermute | solution.py:17
  9.5 5.5 %collective-permute-start.1 = (f32[2,1,32,512]{3,2,1,0:T(8,128)S(1)}, f32[2,1,32,512]{3,2,1,0:T(8,128)S(1)}, u32[]{:S(2)}, u32[]{:S(2)}) collective-permute-start(f32[2,1,32,512]{3,2,1,0:T(8,128)S(1)} %get-tuple-element.22), channel_id=1, source_target_pairs={{0,1},{1,2},{2,3},{3,4},{4,5},{5,6},{6,7},{8,9},{9,10},{10,11},{11... | collective-permute-start | bytes 393224 | tf_op jit(solution)/shard_map/ppermute | solution.py:16
  15.0 1.3 %fusion.24 = (s32[1,1]{1,0:T(1,128)}, s32[1,1]{1,0:T(1,128)}) fusion(s32[1,2]{1,0:T(1,128)} %param.5), kind=kLoop, calls=%fused_computation.101 | loop fusion | bytes 16 | tf_op jit(solution)/shard_map/slice | solution.py:53
  20.2 0.0 copy-start
  20.2 2.3 %dynamic-slice_bitcast_fusion.2 = (f32[8,32,512]{2,1,0:T(8,128)S(1)}, f32[8,32,512]{2,1,0:T(8,128)S(1)}, f32[8,32,512]{2,1,0:T(8,128)S(1)}, f32[8,32,512]{2,1,0:...) fusion(f32[2,3,8,32,512]{4,3,2,1,0:T(8,128)} %param.4, s32[]{:T(128)S(6)} %select_n.19, s32[]{:T(128)S(6)} %add.292, ...), kind=kLoop, calls=%fused_computation.72 | loop fusion | bytes 6291472 | tf_op jit(solution)/shard_map/mul | solution.py:40
  22.5 0.0 copy-start.3
  22.5 0.0 copy-start.5
  22.6 0.0 copy-start.1
  22.6 0.0 collective-permute-done
  22.6 0.0 collective-permute-done.1
  22.6 0.0 copy-done
  22.6 0.6 multiply_subtract_fusion.3
  23.2 0.1 copy-done.3
  23.3 0.2 copy-done.5
  23.5 0.7 multiply_add_fusion.3
  24.2 0.4 fusion.15
  24.6 1.3 %collective-permute-start.2 = (f32[2,1,32,512]{3,2,1,0:T(8,128)S(1)}, f32[2,1,32,512]{3,2,1,0:T(8,128)S(1)}, u32[]{:S(2)}, u32[]{:S(2)}) collective-permute-start(f32[2,1,32,512]{3,2,1,0:T(8,128)S(1)} %get-tuple-element.21), channel_id=1, source_target_pairs={{1,0},{2,1},{3,2},{4,3},{5,4},{6,5},{7,6},{9,8},{10,9},{11,10},{12... | collective-permute-start | bytes 393224 | tf_op jit(solution)/shard_map/ppermute | solution.py:17
  25.9 5.4 %collective-permute-start.3 = (f32[2,1,32,512]{3,2,1,0:T(8,128)S(1)}, f32[2,1,32,512]{3,2,1,0:T(8,128)S(1)}, u32[]{:S(2)}, u32[]{:S(2)}) collective-permute-start(f32[2,1,32,512]{3,2,1,0:T(8,128)S(1)} %get-tuple-element.20), channel_id=1, source_target_pairs={{0,1},{1,2},{2,3},{3,4},{4,5},{5,6},{6,7},{8,9},{9,10},{10,11},{11... | collective-permute-start | bytes 393224 | tf_op jit(solution)/shard_map/ppermute | solution.py:16
  31.4 0.1 pad_maximum_fusion
  31.5 0.9 collective-permute-done.2
  32.4 2.9 %collective-permute-done.3 = f32[2,1,32,512]{3,2,1,0:T(8,128)S(1)} collective-permute-done((f32[2,1,32,512]{3,2,1,0:T(8,128)S(1)}, f32[2,1,32,512]{3,2,1,0:T(8,128)S(1)}, u32[]{:S(2)}, u32[]{:S(2)}) %collective-permute-start.3) | collective-permute-done | bytes 131104 | tf_op jit(solution)/shard_map/ppermute | solution.py:16
  35.4 0.8 multiply_subtract_fusion.2
  36.1 0.0 copy-done.1
  36.2 0.8 multiply_add_fusion.2
  37.0 0.4 fusion.10
  37.4 1.1 pad_maximum_fusion.14
  38.5 1.3 %collective-permute-start.4 = (f32[2,8,32,512]{3,2,1,0:T(8,128)}, f32[2,8,32,512]{3,2,1,0:T(8,128)}, u32[]{:S(2)}, u32[]{:S(2)}) collective-permute-start(f32[2,8,32,512]{3,2,1,0:T(8,128)} %pad_maximum_fusion.14), channel_id=1, source_target_pairs={{8,0},{16,8},{24,16},{9,1},{17,9},{25,17},{10,2},{18,10},{26,18},{... | collective-permute-start | bytes 3145736 | tf_op jit(solution)/shard_map/ppermute | solution.py:25
  39.8 3.6 %collective-permute-done.4 = f32[2,8,32,512]{3,2,1,0:T(8,128)} collective-permute-done((f32[2,8,32,512]{3,2,1,0:T(8,128)}, f32[2,8,32,512]{3,2,1,0:T(8,128)}, u32[]{:S(2)}, u32[]{:S(2)}) %collective-permute-start.4) | collective-permute-done | bytes 1048608 | tf_op jit(solution)/shard_map/ppermute | solution.py:25
  43.3 1.4 %broadcast_select_fusion = f32[2,8,32,512]{3,2,1,0:T(8,128)S(1)} fusion(f32[2,8,32,512]{3,2,1,0:T(8,128)} %collective-permute-done.4, pred[]{:T(512)S(6)} %eq.3, f32[1,2,8,32,512]{4,3,2,1,0:T(8,128)S(1)} %copy-done), kind=kLoop, calls=%fused_computation.93 | loop fusion | flops 262144 | bytes 3145729 | tf_op jit(solution)/shard_map/jit(_where)/select_n | solution.py:67
  44.8 0.0 copy-start.4
  44.8 0.0 copy-start.6
  44.8 1.4 %collective-permute-start.5 = (f32[2,1,32,512]{3,2,1,0:T(8,128)S(1)}, f32[2,1,32,512]{3,2,1,0:T(8,128)S(1)}, u32[]{:S(2)}, u32[]{:S(2)}) collective-permute-start(f32[2,1,32,512]{3,2,1,0:T(8,128)S(1)} %get-tuple-element.19), channel_id=1, source_target_pairs={{1,0},{2,1},{3,2},{4,3},{5,4},{6,5},{7,6},{9,8},{10,9},{11,10},{12... | collective-permute-start | bytes 393224 | tf_op jit(solution)/shard_map/ppermute | solution.py:17
  46.3 5.0 %collective-permute-start.6 = (f32[2,1,32,512]{3,2,1,0:T(8,128)S(1)}, f32[2,1,32,512]{3,2,1,0:T(8,128)S(1)}, u32[]{:S(2)}, u32[]{:S(2)}) collective-permute-start(f32[2,1,32,512]{3,2,1,0:T(8,128)S(1)} %get-tuple-element.18), channel_id=1, source_target_pairs={{0,1},{1,2},{2,3},{3,4},{4,5},{5,6},{6,7},{8,9},{9,10},{10,11},{11... | collective-permute-start | bytes 393224 | tf_op jit(solution)/shard_map/ppermute | solution.py:16
  51.3 1.0 collective-permute-done.5
  52.3 1.8 %collective-permute-done.6 = f32[2,1,32,512]{3,2,1,0:T(8,128)S(1)} collective-permute-done((f32[2,1,32,512]{3,2,1,0:T(8,128)S(1)}, f32[2,1,32,512]{3,2,1,0:T(8,128)S(1)}, u32[]{:S(2)}, u32[]{:S(2)}) %collective-permute-start.6) | collective-permute-done | bytes 131104 | tf_op jit(solution)/shard_map/ppermute | solution.py:16
  54.1 0.6 multiply_subtract_fusion.1
  54.8 0.0 copy-done.4
  54.8 0.0 copy-done.6
  54.8 0.7 multiply_add_fusion.1
  55.5 0.4 fusion.5
  55.9 0.0 copy-start.2
  55.9 1.4 %collective-permute-start.7 = (f32[2,1,32,512]{3,2,1,0:T(8,128)S(1)}, f32[2,1,32,512]{3,2,1,0:T(8,128)S(1)}, u32[]{:S(2)}, u32[]{:S(2)}) collective-permute-start(f32[2,1,32,512]{3,2,1,0:T(8,128)S(1)} %get-tuple-element.17), channel_id=1, source_target_pairs={{1,0},{2,1},{3,2},{4,3},{5,4},{6,5},{7,6},{9,8},{10,9},{11,10},{12... | collective-permute-start | bytes 393224 | tf_op jit(solution)/shard_map/ppermute | solution.py:17
  57.3 5.1 %collective-permute-start.8 = (f32[2,1,32,512]{3,2,1,0:T(8,128)S(1)}, f32[2,1,32,512]{3,2,1,0:T(8,128)S(1)}, u32[]{:S(2)}, u32[]{:S(2)}) collective-permute-start(f32[2,1,32,512]{3,2,1,0:T(8,128)S(1)} %get-tuple-element.16), channel_id=1, source_target_pairs={{0,1},{1,2},{2,3},{3,4},{4,5},{5,6},{6,7},{8,9},{9,10},{10,11},{11... | collective-permute-start | bytes 393224 | tf_op jit(solution)/shard_map/ppermute | solution.py:16
  62.5 0.1 pad_maximum_fusion.1
  62.6 1.9 %collective-permute-done.7 = f32[2,1,32,512]{3,2,1,0:T(8,128)S(1)} collective-permute-done((f32[2,1,32,512]{3,2,1,0:T(8,128)S(1)}, f32[2,1,32,512]{3,2,1,0:T(8,128)S(1)}, u32[]{:S(2)}, u32[]{:S(2)}) %collective-permute-start.7) | collective-permute-done | bytes 131104 | tf_op jit(solution)/shard_map/ppermute | solution.py:17
  64.4 3.0 %collective-permute-done.8 = f32[2,1,32,512]{3,2,1,0:T(8,128)S(1)} collective-permute-done((f32[2,1,32,512]{3,2,1,0:T(8,128)S(1)}, f32[2,1,32,512]{3,2,1,0:T(8,128)S(1)}, u32[]{:S(2)}, u32[]{:S(2)}) %collective-permute-start.8) | collective-permute-done | bytes 131104 | tf_op jit(solution)/shard_map/ppermute | solution.py:16
  67.4 0.0 copy-done.2
  67.4 0.8 multiply_add_fusion
  68.3 0.8 multiply_subtract_fusion
  69.1 1.0 fusion.17
  70.1 0.0 reduce-scatter.2.cloned.1.call-update
  70.1 0.4 add_add_fusion
  70.5 1.1 maximum_bitcast_fusion
  71.6 32.7 %reduce-scatter.2.cloned.1.call-done = f32[8,8,512]{2,1,0:T(8,128)} async-done(((f32[8,32,512]{2,1,0:T(8,128)}), f32[8,8,512]{2,1,0:T(8,128)}) %reduce-scatter.2.cloned.1.call-update) | async-done | bytes 131088 | tf_op jit(solution)/shard_map/reduce_scatter | solution.py:69
  104.2 1.6 %broadcast_multiply_fusion = f32[8,8,512]{2,1,0:T(8,128)} fusion(f32[8,8,512]{2,1,0:T(8,128)} %reduce-scatter.2.cloned.1.call-done), kind=kLoop, calls=%fused_computation.98 | loop fusion | flops 32768 | bytes 262144 | tf_op jit(solution)/shard_map/div | solution.py:69
  (3 shorter events, 0.1 us)
Async XLA Ops:
  7.2 97.1 %reduce-scatter.2.cloned.1.call-start = ((), (), s32[]{:S(2)}) async-start(), calls=%async_computation.1 | async-start | bytes 655360 | tf_op jit(solution)/shard_map/reduce_scatter | solution.py:69
  8.2 14.4 %collective-permute-start = (f32[2,1,32,512]{3,2,1,0:T(8,128)S(1)}, f32[2,1,32,512]{3,2,1,0:T(8,128)S(1)}, u32[]{:S(2)}, u32[]{:S(2)}) collective-permute-start(f32[2,1,32,512]{3,2,1,0:T(8,128)S(1)} %get-tuple-element.23), channel_id=1, source_target_pairs={{1,0},{2,1},{3,2},{4,3},{5,4},{6,5},{7,6},{9,8},{10,9},{11,10},{12... | collective-permute-start | bytes 393224 | tf_op jit(solution)/shard_map/ppermute | solution.py:17
  9.5 13.1 %collective-permute-start.1 = (f32[2,1,32,512]{3,2,1,0:T(8,128)S(1)}, f32[2,1,32,512]{3,2,1,0:T(8,128)S(1)}, u32[]{:S(2)}, u32[]{:S(2)}) collective-permute-start(f32[2,1,32,512]{3,2,1,0:T(8,128)S(1)} %get-tuple-element.22), channel_id=1, source_target_pairs={{0,1},{1,2},{2,3},{3,4},{4,5},{5,6},{6,7},{8,9},{9,10},{10,11},{11... | collective-permute-start | bytes 393224 | tf_op jit(solution)/shard_map/ppermute | solution.py:16
  20.2 2.4 %copy-start = (f32[1,2,8,32,512]{4,3,2,1,0:T(8,128)S(1)}, f32[1,2,8,32,512]{4,3,2,1,0:T(8,128)}, u32[]{:S(2)}) copy-start(f32[1,2,8,32,512]{4,3,2,1,0:T(8,128)} %param.3) | copy-start | bytes 3145732
  22.5 0.8 copy-start.3
  22.5 1.0 copy-start.5
  22.6 13.6 %copy-start.1 = (f32[8,32,512]{2,1,0:T(8,128)}, f32[8,32,512]{2,1,0:T(8,128)S(1)}, u32[]{:S(2)}) copy-start(f32[8,32,512]{2,1,0:T(8,128)S(1)} %get-tuple-element.8) | copy-start | bytes 1572868
  24.6 7.8 %collective-permute-start.2 = (f32[2,1,32,512]{3,2,1,0:T(8,128)S(1)}, f32[2,1,32,512]{3,2,1,0:T(8,128)S(1)}, u32[]{:S(2)}, u32[]{:S(2)}) collective-permute-start(f32[2,1,32,512]{3,2,1,0:T(8,128)S(1)} %get-tuple-element.21), channel_id=1, source_target_pairs={{1,0},{2,1},{3,2},{4,3},{5,4},{6,5},{7,6},{9,8},{10,9},{11,10},{12... | collective-permute-start | bytes 393224 | tf_op jit(solution)/shard_map/ppermute | solution.py:17
  25.9 9.4 %collective-permute-start.3 = (f32[2,1,32,512]{3,2,1,0:T(8,128)S(1)}, f32[2,1,32,512]{3,2,1,0:T(8,128)S(1)}, u32[]{:S(2)}, u32[]{:S(2)}) collective-permute-start(f32[2,1,32,512]{3,2,1,0:T(8,128)S(1)} %get-tuple-element.20), channel_id=1, source_target_pairs={{0,1},{1,2},{2,3},{3,4},{4,5},{5,6},{6,7},{8,9},{9,10},{10,11},{11... | collective-permute-start | bytes 393224 | tf_op jit(solution)/shard_map/ppermute | solution.py:16
  38.5 4.9 %collective-permute-start.4 = (f32[2,8,32,512]{3,2,1,0:T(8,128)}, f32[2,8,32,512]{3,2,1,0:T(8,128)}, u32[]{:S(2)}, u32[]{:S(2)}) collective-permute-start(f32[2,8,32,512]{3,2,1,0:T(8,128)} %pad_maximum_fusion.14), channel_id=1, source_target_pairs={{8,0},{16,8},{24,16},{9,1},{17,9},{25,17},{10,2},{18,10},{26,18},{... | collective-permute-start | bytes 3145736 | tf_op jit(solution)/shard_map/ppermute | solution.py:25
  44.8 9.9 %copy-start.4 = (f32[8,32,512]{2,1,0:T(8,128)S(1)}, f32[8,32,512]{2,1,0:T(8,128)}, u32[]{:S(2)}) copy-start(f32[8,32,512]{2,1,0:T(8,128)} %copy-done.3) | copy-start | bytes 1572868
  44.8 9.9 %copy-start.6 = (f32[8,32,512]{2,1,0:T(8,128)S(1)}, f32[8,32,512]{2,1,0:T(8,128)}, u32[]{:S(2)}) copy-start(f32[8,32,512]{2,1,0:T(8,128)} %copy-done.5) | copy-start | bytes 1572868
  44.8 7.5 %collective-permute-start.5 = (f32[2,1,32,512]{3,2,1,0:T(8,128)S(1)}, f32[2,1,32,512]{3,2,1,0:T(8,128)S(1)}, u32[]{:S(2)}, u32[]{:S(2)}) collective-permute-start(f32[2,1,32,512]{3,2,1,0:T(8,128)S(1)} %get-tuple-element.19), channel_id=1, source_target_pairs={{1,0},{2,1},{3,2},{4,3},{5,4},{6,5},{7,6},{9,8},{10,9},{11,10},{12... | collective-permute-start | bytes 393224 | tf_op jit(solution)/shard_map/ppermute | solution.py:17
  46.3 7.9 %collective-permute-start.6 = (f32[2,1,32,512]{3,2,1,0:T(8,128)S(1)}, f32[2,1,32,512]{3,2,1,0:T(8,128)S(1)}, u32[]{:S(2)}, u32[]{:S(2)}) collective-permute-start(f32[2,1,32,512]{3,2,1,0:T(8,128)S(1)} %get-tuple-element.18), channel_id=1, source_target_pairs={{0,1},{1,2},{2,3},{3,4},{4,5},{5,6},{6,7},{8,9},{9,10},{10,11},{11... | collective-permute-start | bytes 393224 | tf_op jit(solution)/shard_map/ppermute | solution.py:16
  55.9 11.5 %copy-start.2 = (f32[8,32,512]{2,1,0:T(8,128)S(1)}, f32[8,32,512]{2,1,0:T(8,128)}, u32[]{:S(2)}) copy-start(f32[8,32,512]{2,1,0:T(8,128)} %copy-done.1) | copy-start | bytes 1572868
  55.9 8.5 %collective-permute-start.7 = (f32[2,1,32,512]{3,2,1,0:T(8,128)S(1)}, f32[2,1,32,512]{3,2,1,0:T(8,128)S(1)}, u32[]{:S(2)}, u32[]{:S(2)}) collective-permute-start(f32[2,1,32,512]{3,2,1,0:T(8,128)S(1)} %get-tuple-element.17), channel_id=1, source_target_pairs={{1,0},{2,1},{3,2},{4,3},{5,4},{6,5},{7,6},{9,8},{10,9},{11,10},{12... | collective-permute-start | bytes 393224 | tf_op jit(solution)/shard_map/ppermute | solution.py:17
  57.3 10.1 %collective-permute-start.8 = (f32[2,1,32,512]{3,2,1,0:T(8,128)S(1)}, f32[2,1,32,512]{3,2,1,0:T(8,128)S(1)}, u32[]{:S(2)}, u32[]{:S(2)}) collective-permute-start(f32[2,1,32,512]{3,2,1,0:T(8,128)S(1)} %get-tuple-element.16), channel_id=1, source_target_pairs={{0,1},{1,2},{2,3},{3,4},{4,5},{5,6},{6,7},{8,9},{9,10},{10,11},{11... | collective-permute-start | bytes 393224 | tf_op jit(solution)/shard_map/ppermute | solution.py:16
Sparse Core Ops, SparseCore 0:
  70.2 33.9 reduce-scatter.1
where the time goes:
time: 113 us
  waiting for transfers between devices  47.8 us (42%)
  starting transfers between devices  27.8 us (25%)
  between operations  18.2 us (16%)
  other arithmetic  13.8 us (12%)
  local copies, waits for them, and re-layouts  4.99 us (4%)
    reduce_scatter x1, waiting for transfers between devices, body(): lax.psum_scatter(total, 'tm', scatter_dimension=1, tiled=True)  32.7 us
    ppermute x4, starting transfers between devices, with_halo(): before = lax.ppermute(last, axis, up)  21.1 us
    ppermute x4, waiting for transfers between devices, with_halo(): before = lax.ppermute(last, axis, up)  7.76 us
    ppermute x4, starting transfers between devices, with_halo(): after = lax.ppermute(first, axis, down)  5.43 us
    ppermute x4, waiting for transfers between devices, with_halo(): after = lax.ppermute(first, axis, down)  3.79 us
    ppermute x1, waiting for transfers between devices, passed_along(): return lax.ppermute(array, axis, pairs)  3.59 us
    add x4, other arithmetic, advance(): flow[0] * (east_side - west_side) + flow[1] * (north_side - south_side)  3.06 us
    sub x4, other arithmetic, advance(): east_side + west_side + north_side + south_side + upper_side + lower_side  2.82 us
  transfers between devices with their start and end apart: 10, of which 8 were waited for; matrix products, arithmetic and copies ran while one was open for 5% of the time, Pallas kernels for 0%

commit v1 on v0

v1 whole, which is shorter than its diff:
```python
import functools

import jax
import jax.numpy as jnp
from jax import lax
from jax.experimental import pallas as pl
from jax.experimental.pallas import tpu as pltpu
from jax.sharding import PartitionSpec as P

coupling = 0.3
MESH = pl.DeviceIdType.MESH


def shifted(field):
    rows, lanes = field.shape
    row = lax.broadcasted_iota(jnp.int32, field.shape, 0)
    lane = lax.broadcasted_iota(jnp.int32, field.shape, 1)
    north = jnp.where(row == rows - 1, 0.0, pltpu.roll(field, rows - 1, 0))
    south = jnp.where(row == 0, 0.0, pltpu.roll(field, 1, 0))
    upper = jnp.where(lane == lanes - 1, 0.0, pltpu.roll(field, lanes - 1, 1))
    lower = jnp.where(lane == 0, 0.0, pltpu.roll(field, 1, 1))
    return north, south, upper, lower


def moved(west, centre, east, u, v, w, rate):
    north, south, upper, lower = shifted(centre)
    around = (east + west) + (north + south) + (upper + lower)
    transport = u * (east - west) + v * (north - south) + w * (upper - lower)
    return (1.0 - 6.0 * rate) * centre + rate * around + 0.25 * transport


def layer_step(src, flow, snap, layer):
    u, v, w = (flow[snap, c, layer] for c in range(3))
    a, b = src[0, layer + 1], src[1, layer + 1]
    temper = moved(src[0, layer], a, src[0, layer + 2], u, v, w, 0.14) + coupling * b
    dopant = moved(src[1, layer], b, src[1, layer + 2], u, v, w, 0.06)
    return temper, dopant


def kernel(
    slabs, blocks, state, velocity, snaps, out, grad,
    x0, x1, x2, y0, y1, y2, flow, total, from_mate, from_early, from_late,
    load_sem, halo_send, halo_recv, pass_send, pass_recv, grad_send, grad_recv, out_sem,
):
    t, s = lax.axis_index("tm"), lax.axis_index("space")
    depth = x2.shape[1]
    pairs = depth // 2
    steps = snaps.shape[1]
    has_up, has_down = s < blocks - 1, s > 0
    first_phase, second_phase = t > 0, t < slabs - 1

    load_state = pltpu.make_async_copy(state, x0.at[:, pl.ds(1, depth)], load_sem.at[0])
    load_flow = pltpu.make_async_copy(velocity, flow, load_sem.at[1])

    @pl.when(first_phase)
    def _():
        load_state.start()

    load_flow.start()

    barrier = pltpu.get_barrier_semaphore()

    def greet(target):
        pl.semaphore_signal(barrier, inc=1, device_id=target, device_id_type=MESH)

    for other in range(1, slabs):
        greet({"tm": lax.rem(t + other, slabs)})
    pl.when(has_up)(lambda: greet({"space": s + 1}))
    pl.when(has_down)(lambda: greet({"space": s - 1}))
    ends = jnp.where(has_up, 0, 1) + jnp.where(has_down, 0, 1)
    pl.semaphore_wait(barrier, slabs + 1 - ends)

    def halo(k, buf, source=None):
        low, high = (buf.at[:, 1], buf.at[:, depth]) if source is None else (source.at[:, 0], source.at[:, depth - 1])
        up = pltpu.make_async_remote_copy(
            high, buf.at[:, 0], halo_send.at[k, 0], halo_recv.at[k, 0], {"space": s + 1}, MESH)
        down = pltpu.make_async_remote_copy(
            low, buf.at[:, depth + 1], halo_send.at[k, 1], halo_recv.at[k, 1], {"space": s - 1}, MESH)
        return up, down

    def send_halo(pair):
        pl.when(has_up)(lambda: pair[0].start())
        pl.when(has_down)(lambda: pair[1].start())

    def recv_halo(pair):
        pl.when(has_down)(lambda: pair[0].wait_recv())
        pl.when(has_up)(lambda: pair[1].wait_recv())

    def sent_halo(pair):
        pl.when(has_up)(lambda: pair[0].wait_send())
        pl.when(has_down)(lambda: pair[1].wait_send())

    def clear_ends(*bufs):
        for buf in bufs:
            @pl.when(s == 0)
            def _(buf=buf):
                buf[:, 0] = jnp.zeros(buf.shape[:1] + buf.shape[2:], jnp.float32)

            @pl.when(s == blocks - 1)
            def _(buf=buf):
                buf[:, depth + 1] = jnp.zeros(buf.shape[:1] + buf.shape[2:], jnp.float32)

    halo0, halo1, halo2, halo3 = halo(0, x0, state), halo(1, x1), halo(2, y0), halo(3, y1)

    def passing(layer, target):
        return pltpu.make_async_remote_copy(
            x2.at[:, layer], y0.at[:, layer + 1], pass_send.at[layer], pass_recv.at[layer], {"tm": target}, MESH)

    def step_into(src, dst, offset, snap, p, summed=False):
        for layer in (p, depth - 1 - p):
            temper, dopant = layer_step(src, flow, snap, layer)
            dst[0, layer + offset] = temper
            dst[1, layer + offset] = dopant
            if summed:
                total[layer] = src[0, layer + 1] + temper

    @pl.when(first_phase)
    def _():
        send_halo(halo0)
        clear_ends(x0, x1)
        load_state.wait()

    load_flow.wait()

    @pl.when(first_phase)
    def _():
        @pl.loop(0, pairs)
        def _(i):
            p = pairs - 1 - i

            @pl.when(p == 0)
            def _():
                recv_halo(halo0)

            step_into(x0, x1, 1, snaps[0, steps - 1], p)

        send_halo(halo1)

        @pl.loop(0, pairs)
        def _(i):
            p = pairs - 1 - i

            @pl.when(p == 0)
            def _():
                recv_halo(halo1)

            step_into(x1, x2, 0, snaps[0, 0], p, summed=True)

            @pl.when(p == pairs - 1)
            def _():
                passing(p, t - 1).start()
                passing(depth - 1 - p, t - 1).start()

        @pl.loop(0, pairs - 1)
        def _(p):
            passing(p, t - 1).start()
            passing(depth - 1 - p, t - 1).start()

    @pl.when(second_phase)
    def _():
        clear_ends(y0, y1)

        def arrived(p):
            passing(p, t + 1).wait_recv()
            passing(depth - 1 - p, t + 1).wait_recv()

        arrived(0)
        send_halo(halo2)
        slow = t == 1

        @pl.when(jnp.logical_not(slow))
        def _():
            for p in range(1, pairs):
                arrived(p)

        @pl.loop(0, pairs)
        def _(i):
            p = lax.rem(i + jnp.where(slow, 0, 1), pairs)

            @pl.when(jnp.logical_and(slow, i < pairs - 1))
            def _():
                arrived(i + 1)

            @pl.when(p == 0)
            def _():
                recv_halo(halo2)

            step_into(y0, y1, 1, snaps[0, steps - 1], p)

            @pl.when(p == 0)
            def _():
                send_halo(halo3)

        @pl.loop(0, pairs)
        def _(i):
            p = pairs - 1 - i

            @pl.when(p == 0)
            def _():
                recv_halo(halo3)

            step_into(y1, y2, 0, snaps[0, 0], p, summed=True)

    store_mid = pltpu.make_async_copy(y2, out, out_sem)
    store_end = pltpu.make_async_copy(x2, out, out_sem)
    pl.when(second_phase)(lambda: store_mid.start())
    pl.when(t == slabs - 1)(lambda: store_end.start())

    rows = total.shape[1] // slabs

    def share(first, count, dst, slot, target):
        return pltpu.make_async_remote_copy(
            total.at[:, pl.ds(first * rows, count * rows)], dst, grad_send.at[target], grad_recv.at[slot],
            {"tm": target}, MESH)

    mate0 = share(1, 3, from_mate, 0, 1)
    mate3 = share(0, 3, from_mate, 0, 2)
    back1 = share(0, 1, from_late, 2, 0)
    back2 = share(3, 1, from_late, 2, 3)
    cross20 = share(0, 1, from_early, 1, 0)
    cross21 = share(1, 1, from_early, 1, 1)
    cross12 = share(2, 1, from_early, 1, 2)
    cross13 = share(3, 1, from_early, 1, 3)

    def mine(index):
        return total[:, index * rows:(index + 1) * rows]

    scale = 1.0 / steps

    @pl.when(t == 0)
    def _():
        mate0.start()
        cross20.wait_recv()
        back1.wait_recv()
        grad[...] = (mine(0) + from_late[...] + from_early[...]) * scale
        mate0.wait_send()

    @pl.when(t == 1)
    def _():
        mate0.wait_recv()
        total[:, rows:] += from_mate[...]
        cross12.start()
        cross13.start()
        back1.start()
        cross21.wait_recv()
        grad[...] = (mine(1) + from_early[...]) * scale
        cross12.wait_send()
        cross13.wait_send()
        back1.wait_send()

    @pl.when(t == 2)
    def _():
        mate3.wait_recv()
        total[:, :3 * rows] += from_mate[...]
        cross20.start()
        cross21.start()
        back2.start()
        cross12.wait_recv()
        grad[...] = (mine(2) + from_early[...]) * scale
        cross20.wait_send()
        cross21.wait_send()
        back2.wait_send()

    @pl.when(t == 3)
    def _():
        mate3.start()
        back2.wait_recv()
        cross13.wait_recv()
        grad[...] = (mine(3) + from_late[...] + from_early[...]) * scale
        mate3.wait_send()

    @pl.when(first_phase)
    def _():
        sent_halo(halo0)
        sent_halo(halo1)

        @pl.loop(0, depth)
        def _(layer):
            passing(layer, t - 1).wait_send()

    @pl.when(second_phase)
    def _():
        sent_halo(halo2)
        sent_halo(halo3)
        store_mid.wait()

    pl.when(t == slabs - 1)(lambda: store_end.wait())


def body(slabs, blocks, slab_states, velocity, snap_of_step):
    state = slab_states[0]
    fields, depth, ny, nz = state.shape
    rows = ny // slabs
    f32 = jnp.float32
    widened = pltpu.VMEM((fields, depth + 2, ny, nz), f32)
    plain = pltpu.VMEM((fields, depth, ny, nz), f32)
    dma = pltpu.SemaphoreType.DMA
    final, gradient = pl.pallas_call(
        functools.partial(kernel, slabs, blocks),
        out_shape=(
            jax.ShapeDtypeStruct(state.shape, f32),
            jax.ShapeDtypeStruct((depth, rows, nz), f32),
        ),
        in_specs=[
            pl.BlockSpec(memory_space=pl.ANY),
            pl.BlockSpec(memory_space=pl.ANY),
            pl.BlockSpec(memory_space=pltpu.SMEM),
        ],
        out_specs=(pl.BlockSpec(memory_space=pl.ANY), pl.BlockSpec(memory_space=pltpu.VMEM)),
        scratch_shapes=[
            widened, widened, plain, widened, widened, plain,
            pltpu.VMEM(velocity.shape, f32),
            pltpu.VMEM((depth, ny, nz), f32),
            pltpu.VMEM((depth, 3 * rows, nz), f32),
            pltpu.VMEM((depth, rows, nz), f32),
            pltpu.VMEM((depth, rows, nz), f32),
            dma((2,)), dma((4, 2)), dma((4, 2)), dma((depth,)), dma((depth,)), dma((slabs,)), dma((3,)), dma,
        ],
        compiler_params=pltpu.CompilerParams(
            collective_id=0, has_side_effects=True, vmem_limit_bytes=32 * 1024 * 1024),
        cost_estimate=pl.CostEstimate(flops=200 * state.size, bytes_accessed=28 * state.size, transcendentals=0),
    )(state, velocity, snap_of_step)
    return final[None], gradient


def solution(mesh):
    placed = (P("tm", None, "space", None, None), P(None, None, "space", None, None), P("tm", None))
    return jax.shard_map(
        functools.partial(body, mesh.shape["tm"], mesh.shape["space"]),
        mesh=mesh,
        in_specs=placed,
        out_specs=(P("tm", None, "space", None, None), P("space", "tm", None)),
        check_vma=False,
    )
```

time: 113 us -> 43.7 us (0.39)
  the two profiles are of different devices: /device:TPU:0 before, /device:TPU:23 now
where the time goes in v1:
time: 43.7 us; the launch traced here: 43.5 us
  Pallas kernels  37.5 us (86%)
  local copies, waits for them, and re-layouts  5.39 us (12%)
  between operations  0.65 us (1%)
    pallas_call x1, Pallas kernels, body(): pl.pallas_call(functools.partial(kernel, slabs, blocks), out_shape=(jax.S...  37.5 us
    unnamed x8, local copies, waits for them, and re-layouts  5.39 us

profile of v1, /device:TPU:23, one launch (start us, length us, event | category | flops | bytes accessed | tf_op | source)
XLA Modules:
  0.0 43.5 jit_solution(15996770759579388206)
XLA Ops:
  0.6 0.0 copy-start
  0.6 1.9 %copy-done = f32[2,3,8,32,512]{4,3,2,1,0:T(8,128)S(1)} copy-done((f32[2,3,8,32,512]{4,3,2,1,0:T(8,128)S(1)}, f32[2,3,8,32,512]{4,3,2,1,0:T(8,128)}, u32[]{:S(2)}) %copy-start) | copy-done | bytes 3145752
  2.5 0.0 copy-start.1
  2.5 1.2 %copy-done.1 = f32[1,2,8,32,512]{4,3,2,1,0:T(8,128)S(1)} copy-done((f32[1,2,8,32,512]{4,3,2,1,0:T(8,128)S(1)}, f32[1,2,8,32,512]{4,3,2,1,0:T(8,128)}, u32[]{:S(2)}) %copy-start.1) | copy-done | bytes 1048600
  3.7 0.0 copy-start.2
  3.7 0.7 %copy-done.2 = s32[1,2]{1,0:T(1,128)S(1)} copy-done((s32[1,2]{1,0:T(1,128)S(1)}, s32[1,2]{1,0:T(1,128)}, u32[]{:S(2)}) %copy-start.2) | copy-done | bytes 32
  4.4 37.5 %shard_map.50 = (f32[2,8,32,512]{3,2,1,0:T(8,128)S(1)}, f32[8,8,512]{2,1,0:T(8,128)S(1)}) custom-call(f32[2,8,32,512]{3,2,1,0:T(8,128)S(1)} %bitcast.2, f32[2,3,8,32,512]{4,3,2,1,0:T(8,128)S(1)} %copy-done, s32[1,2]{1,0:T(1,128)S(1)} %copy-done.2), custom_call_target="tpu_custom_call" | custom-call | flops 52428800 | bytes 7340032 | tf_op jit(solution)/shard_map/pallas_call | solution.py:298
  41.9 1.0 %copy.7 = f32[1,2,8,32,512]{4,3,2,1,0:T(8,128)} copy(f32[1,2,8,32,512]{4,3,2,1,0:T(8,128)S(1)} %bitcast.3) | data formatting | bytes 2097152
  42.9 0.7 %copy.8 = f32[8,8,512]{2,1,0:T(8,128)} copy(f32[8,8,512]{2,1,0:T(8,128)S(1)} %get-tuple-element.9) | data formatting | bytes 262144
Async XLA Ops:
  0.6 1.9 %copy-start = (f32[2,3,8,32,512]{4,3,2,1,0:T(8,128)S(1)}, f32[2,3,8,32,512]{4,3,2,1,0:T(8,128)}, u32[]{:S(2)}) copy-start(f32[2,3,8,32,512]{4,3,2,1,0:T(8,128)} %velocity.1) | copy-start | bytes 9437188
  2.5 1.2 %copy-start.1 = (f32[1,2,8,32,512]{4,3,2,1,0:T(8,128)S(1)}, f32[1,2,8,32,512]{4,3,2,1,0:T(8,128)}, u32[]{:S(2)}) copy-start(f32[1,2,8,32,512]{4,3,2,1,0:T(8,128)} %param.3) | copy-start | bytes 3145732
  3.7 0.7 %copy-start.2 = (s32[1,2]{1,0:T(1,128)S(1)}, s32[1,2]{1,0:T(1,128)}, u32[]{:S(2)}) copy-start(s32[1,2]{1,0:T(1,128)} %snaps.1) | copy-start | bytes 28

commit v2 on v1

--- a/solution.py
+++ b/solution.py
@@ -65,18 +65,24 @@
 
     for other in range(1, slabs):
         greet({"tm": lax.rem(t + other, slabs)})
-    pl.when(has_up)(lambda: greet({"space": s + 1}))
-    pl.when(has_down)(lambda: greet({"space": s - 1}))
-    ends = jnp.where(has_up, 0, 1) + jnp.where(has_down, 0, 1)
-    pl.semaphore_wait(barrier, slabs + 1 - ends)
-
-    def halo(k, buf, source=None):
-        low, high = (buf.at[:, 1], buf.at[:, depth]) if source is None else (source.at[:, 0], source.at[:, depth - 1])
-        up = pltpu.make_async_remote_copy(
-            high, buf.at[:, 0], halo_send.at[k, 0], halo_recv.at[k, 0], {"space": s + 1}, MESH)
-        down = pltpu.make_async_remote_copy(
-            low, buf.at[:, depth + 1], halo_send.at[k, 1], halo_recv.at[k, 1], {"space": s - 1}, MESH)
-        return up, down
+    for by, there in ((1, has_up), (-1, has_down)):
+        @pl.when(there)
+        def _(by=by):
+            greet({"space": s + by})
+            pl.when(first_phase)(lambda: greet({"tm": t - 1, "space": s + by}))
+            pl.when(second_phase)(lambda: greet({"tm": t + 1, "space": s + by}))
+
+    sides = jnp.where(has_up, 1, 0) + jnp.where(has_down, 1, 0)
+    rounds = 1 + jnp.where(first_phase, 1, 0) + jnp.where(second_phase, 1, 0)
+    pl.semaphore_wait(barrier, slabs - 1 + sides * rounds)
+
+    def halo(k, low, high, buf, to=0):
+        def copy(source, layer, side, by):
+            return pltpu.make_async_remote_copy(
+                source, buf.at[:, layer], halo_send.at[k, side], halo_recv.at[k, side],
+                {"tm": t + to, "space": s + by}, MESH)
+
+        return copy(high, 0, 0, 1), copy(low, depth + 1, 1, -1)
 
     def send_halo(pair):
         pl.when(has_up)(lambda: pair[0].start())
@@ -100,7 +106,10 @@
             def _(buf=buf):
                 buf[:, depth + 1] = jnp.zeros(buf.shape[:1] + buf.shape[2:], jnp.float32)
 
-    halo0, halo1, halo2, halo3 = halo(0, x0, state), halo(1, x1), halo(2, y0), halo(3, y1)
+    halo0 = halo(0, state.at[:, 0], state.at[:, depth - 1], x0)
+    halo1 = halo(1, x1.at[:, 1], x1.at[:, depth], x1)
+    halo2 = halo(2, x2.at[:, 0], x2.at[:, depth - 1], y0, -1)
+    halo3 = halo(3, y1.at[:, 1], y1.at[:, depth], y1)
 
     def passing(layer, target):
         return pltpu.make_async_remote_copy(
@@ -151,11 +160,73 @@
                 passing(p, t - 1).start()
                 passing(depth - 1 - p, t - 1).start()
 
+        send_halo(halo2)
+
         @pl.loop(0, pairs - 1)
         def _(p):
             passing(p, t - 1).start()
             passing(depth - 1 - p, t - 1).start()
 
+    rows = total.shape[1] // slabs
+    parts = ((1, depth - 2), (0, 1), (depth - 1, 1))
+    inner, outer = (0,), (1, 2)
+
+    class Share:
+        def __init__(self, first, count, dst, slot, target):
+            self.copies = [
+                pltpu.make_async_remote_copy(
+                    total.at[pl.ds(layer, layers), pl.ds(first * rows, count * rows)],
+                    dst.at[pl.ds(layer, layers)], grad_send.at[target, part], grad_recv.at[slot, part],
+                    {"tm": target}, MESH)
+                for part, (layer, layers) in enumerate(parts)
+            ]
+
+        def start(self, which=inner + outer):
+            for part in which:
+                self.copies[part].start()
+
+        def wait_recv(self):
+            for copy in self.copies:
+                copy.wait_recv()
+
+        def wait_send(self):
+            for copy in self.copies:
+                copy.wait_send()
+
+    mate0 = Share(1, 3, from_mate, 0, 1)
+    mate3 = Share(0, 3, from_mate, 0, 2)
+    back1 = Share(0, 1, from_late, 2, 0)
+    back2 = Share(3, 1, from_late, 2, 3)
+    cross20 = Share(0, 1, from_early, 1, 0)
+    cross21 = Share(1, 1, from_early, 1, 1)
+    cross12 = Share(2, 1, from_early, 1, 2)
+    cross13 = Share(3, 1, from_early, 1, 3)
+
+    def give(which):
+        @pl.when(t == 0)
+        def _():
+            mate0.start(which)
+
+        @pl.when(t == 1)
+        def _():
+            if which == inner:
+                mate0.wait_recv()
+            for layer, layers in (parts[part] for part in which):
+                total[layer:layer + layers, rows:] += from_mate[layer:layer + layers]
+            for each in (cross12, cross13, back1):
+                each.start(which)
+
+        @pl.when(t == 2)
+        def _():
+            if which == inner:
+                mate3.wait_recv()
+            for layer, layers in (parts[part] for part in which):
+                total[layer:layer + layers, :3 * rows] += from_mate[layer:layer + layers]
+            for each in (cross20, cross21, back2):
+                each.start(which)
+
+    pl.when(t == slabs - 1)(lambda: mate3.start())
+
     @pl.when(second_phase)
     def _():
         clear_ends(y0, y1)
@@ -165,7 +236,6 @@
             passing(depth - 1 - p, t + 1).wait_recv()
 
         arrived(0)
-        send_halo(halo2)
         slow = t == 1
 
         @pl.when(jnp.logical_not(slow))
@@ -197,31 +267,18 @@
 
             @pl.when(p == 0)
             def _():
+                give(inner)
                 recv_halo(halo3)
 
             step_into(y1, y2, 0, snaps[0, 0], p, summed=True)
+
+        give(outer)
 
     store_mid = pltpu.make_async_copy(y2, out, out_sem)
     store_end = pltpu.make_async_copy(x2, out, out_sem)
     pl.when(second_phase)(lambda: store_mid.start())
     pl.when(t == slabs - 1)(lambda: store_end.start())
 
-    rows = total.shape[1] // slabs
-
-    def share(first, count, dst, slot, target):
-        return pltpu.make_async_remote_copy(
-            total.at[:, pl.ds(first * rows, count * rows)], dst, grad_send.at[target], grad_recv.at[slot],
-            {"tm": target}, MESH)
-
-    mate0 = share(1, 3, from_mate, 0, 1)
-    mate3 = share(0, 3, from_mate, 0, 2)
-    back1 = share(0, 1, from_late, 2, 0)
-    back2 = share(3, 1, from_late, 2, 3)
-    cross20 = share(0, 1, from_early, 1, 0)
-    cross21 = share(1, 1, from_early, 1, 1)
-    cross12 = share(2, 1, from_early, 1, 2)
-    cross13 = share(3, 1, from_early, 1, 3)
-
     def mine(index):
         return total[:, index * rows:(index + 1) * rows]
 
@@ -229,7 +286,6 @@
 
     @pl.when(t == 0)
     def _():
-        mate0.start()
         cross20.wait_recv()
         back1.wait_recv()
         grad[...] = (mine(0) + from_late[...] + from_early[...]) * scale
@@ -237,11 +293,6 @@
 
     @pl.when(t == 1)
     def _():
-        mate0.wait_recv()
-        total[:, rows:] += from_mate[...]
-        cross12.start()
-        cross13.start()
-        back1.start()
         cross21.wait_recv()
         grad[...] = (mine(1) + from_early[...]) * scale
         cross12.wait_send()
@@ -250,11 +301,6 @@
 
     @pl.when(t == 2)
     def _():
-        mate3.wait_recv()
-        total[:, :3 * rows] += from_mate[...]
-        cross20.start()
-        cross21.start()
-        back2.start()
         cross12.wait_recv()
         grad[...] = (mine(2) + from_early[...]) * scale
         cross20.wait_send()
@@ -263,7 +309,6 @@
 
     @pl.when(t == 3)
     def _():
-        mate3.start()
         back2.wait_recv()
         cross13.wait_recv()
         grad[...] = (mine(3) + from_late[...] + from_early[...]) * scale
@@ -273,6 +318,7 @@
     def _():
         sent_halo(halo0)
         sent_halo(halo1)
+        sent_halo(halo2)
 
         @pl.loop(0, depth)
         def _(layer):
@@ -280,7 +326,6 @@
 
     @pl.when(second_phase)
     def _():
-        sent_halo(halo2)
         sent_halo(halo3)
         store_mid.wait()
 
@@ -314,10 +359,10 @@
             pltpu.VMEM((depth, 3 * rows, nz), f32),
             pltpu.VMEM((depth, rows, nz), f32),
             pltpu.VMEM((depth, rows, nz), f32),
-            dma((2,)), dma((4, 2)), dma((4, 2)), dma((depth,)), dma((depth,)), dma((slabs,)), dma((3,)), dma,
+            dma((2,)), dma((4, 2)), dma((4, 2)), dma((depth,)), dma((depth,)), dma((slabs, 3)), dma((3, 3)), dma,
         ],
         compiler_params=pltpu.CompilerParams(
-            collective_id=0, has_side_effects=True, vmem_limit_bytes=32 * 1024 * 1024),
+            collective_id=0, has_side_effects=True, vmem_limit_bytes=60 * 1024 * 1024),
         cost_estimate=pl.CostEstimate(flops=200 * state.size, bytes_accessed=28 * state.size, transcendentals=0),
     )(state, velocity, snap_of_step)
     return final[None], gradient

time: 43.7 us -> 43.8 us (level)
  the two profiles are of different devices: /device:TPU:23 before, /device:TPU:21 now
where the time goes in v2:
time: 43.8 us; the launch traced here: 43.3 us
  Pallas kernels  38.8 us (89%)
  local copies, waits for them, and re-layouts  3.86 us (9%)
  between operations  0.64 us (1%)
    pallas_call x1, Pallas kernels, body(): pl.pallas_call(functools.partial(kernel, slabs, blocks), out_shape=(jax.S...  38.8 us
    unnamed x2, local copies, waits for them, and re-layouts  3.86 us

profile of v2, /device:TPU:21, one launch (start us, length us, event | category | flops | bytes accessed | tf_op | source)
XLA Modules:
  0.0 43.3 jit_solution(1949120446268547599)
XLA Ops:
  0.6 38.8 %shard_map.50 = (f32[2,8,32,512]{3,2,1,0:T(8,128)}, f32[8,8,512]{2,1,0:T(8,128)}) custom-call(f32[2,8,32,512]{3,2,1,0:T(8,128)} %bitcast.2, f32[2,3,8,32,512]{4,3,2,1,0:T(8,128)} %velocity.1, s32[1,2]{1,0:T(1,128)} %snaps.1), custom_call_target="tpu_custom_call" | custom-call | flops 52428800 | bytes 7340032 | tf_op jit(solution)/shard_map/pallas_call | solution.py:343
  39.5 2.3 %copy.7 = f32[1,2,8,32,512]{4,3,2,1,0:T(8,128)} copy(f32[1,2,8,32,512]{4,3,2,1,0:T(8,128)} %bitcast.3) | data formatting | bytes 2097152
  41.8 1.6 %copy.8 = f32[8,8,512]{2,1,0:T(8,128)} copy(f32[8,8,512]{2,1,0:T(8,128)} %get-tuple-element.9) | data formatting | bytes 262144

commit v3 on v2

--- a/solution.py
+++ b/solution.py
@@ -29,18 +29,30 @@
     return (1.0 - 6.0 * rate) * centre + rate * around + 0.25 * transport
 
 
-def layer_step(src, flow, snap, layer):
-    u, v, w = (flow[snap, c, layer] for c in range(3))
+def flow_at(flow, snap, layer):
+    return tuple(flow[snap, c, layer] for c in range(3))
+
+
+def flow_picked(flow, pick, layer):
+    rows, lanes = flow.shape[3:]
+    pick = jnp.concatenate([pick] * (lanes // pick.shape[1]), axis=1)
+    pick = jnp.concatenate([pick] * (rows // pick.shape[0]), axis=0)
+    return tuple(jnp.where(pick > 0.5, flow[1, c, layer], flow[0, c, layer]) for c in range(3))
+
+
+def temper_step(src, flows, layer):
     a, b = src[0, layer + 1], src[1, layer + 1]
-    temper = moved(src[0, layer], a, src[0, layer + 2], u, v, w, 0.14) + coupling * b
-    dopant = moved(src[1, layer], b, src[1, layer + 2], u, v, w, 0.06)
-    return temper, dopant
+    return moved(src[0, layer], a, src[0, layer + 2], *flows, 0.14) + coupling * b
+
+
+def dopant_step(src, flows, layer):
+    return moved(src[1, layer], src[1, layer + 1], src[1, layer + 2], *flows, 0.06)
 
 
 def kernel(
-    slabs, blocks, state, velocity, snaps, out, grad,
-    x0, x1, x2, y0, y1, y2, flow, total, from_mate, from_early, from_late,
-    load_sem, halo_send, halo_recv, pass_send, pass_recv, grad_send, grad_recv, out_sem,
+    slabs, blocks, state, velocity, snaps_in, out, grad,
+    x0, x1, x2, y0, y1, y2, flow, total, from_mate, from_early, from_late, snaps, pick_out, pick,
+    load_sem, halo_send, halo_recv, pass_send, pass_recv, raw_send, raw_recv, grad_send, grad_recv, out_sem,
 ):
     t, s = lax.axis_index("tm"), lax.axis_index("space")
     depth = x2.shape[1]
@@ -48,9 +60,14 @@
     steps = snaps.shape[1]
     has_up, has_down = s < blocks - 1, s > 0
     first_phase, second_phase = t > 0, t < slabs - 1
+    mate = t + 1 - 2 * lax.rem(t, 2)
+    source = slabs // 2
 
     load_state = pltpu.make_async_copy(state, x0.at[:, pl.ds(1, depth)], load_sem.at[0])
     load_flow = pltpu.make_async_copy(velocity, flow, load_sem.at[1])
+    load_snaps = pltpu.make_async_copy(snaps_in, snaps, load_sem.at[2])
+
+    load_snaps.start()
 
     @pl.when(first_phase)
     def _():
@@ -76,11 +93,11 @@
     rounds = 1 + jnp.where(first_phase, 1, 0) + jnp.where(second_phase, 1, 0)
     pl.semaphore_wait(barrier, slabs - 1 + sides * rounds)
 
-    def halo(k, low, high, buf, to=0):
+    def halo(k, field, low, high, buf, tm=t):
         def copy(source, layer, side, by):
             return pltpu.make_async_remote_copy(
-                source, buf.at[:, layer], halo_send.at[k, side], halo_recv.at[k, side],
-                {"tm": t + to, "space": s + by}, MESH)
+                source, buf.at[field, layer], halo_send.at[k, field, side], halo_recv.at[k, field, side],
+                {"tm": tm, "space": s + by}, MESH)
 
         return copy(high, 0, 0, 1), copy(low, depth + 1, 1, -1)
 
@@ -106,44 +123,82 @@
             def _(buf=buf):
                 buf[:, depth + 1] = jnp.zeros(buf.shape[:1] + buf.shape[2:], jnp.float32)
 
-    halo0 = halo(0, state.at[:, 0], state.at[:, depth - 1], x0)
-    halo1 = halo(1, x1.at[:, 1], x1.at[:, depth], x1)
-    halo2 = halo(2, x2.at[:, 0], x2.at[:, depth - 1], y0, -1)
-    halo3 = halo(3, y1.at[:, 1], y1.at[:, depth], y1)
-
-    def passing(layer, target):
+    A, B = 0, 1
+    halo0 = [halo(0, f, state.at[f, 0], state.at[f, depth - 1], x0) for f in (A, B)]
+    relay0 = halo(0, B, x0.at[B, 1], x0.at[B, depth], x0)
+    halo1 = [halo(1, f, x1.at[f, 1], x1.at[f, depth], x1) for f in (A, B)]
+    halo2 = [halo(2, f, x2.at[f, 0], x2.at[f, depth - 1], y0, (t - 1, mate)[f]) for f in (A, B)]
+    halo3 = [halo(3, f, y1.at[f, 1], y1.at[f, depth], y1) for f in (A, B)]
+
+    def passing(field, layer, target):
         return pltpu.make_async_remote_copy(
-            x2.at[:, layer], y0.at[:, layer + 1], pass_send.at[layer], pass_recv.at[layer], {"tm": target}, MESH)
+            x2.at[field, layer], y0.at[field, layer + 1], pass_send.at[field, layer], pass_recv.at[field, layer],
+            {"tm": target}, MESH)
+
+    def pass_pair(field, p, target):
+        passing(field, p, target).start()
+        passing(field, depth - 1 - p, target).start()
+
+    def arrived(field, p, origin):
+        passing(field, p, origin).wait_recv()
+        passing(field, depth - 1 - p, origin).wait_recv()
+
+    def raw(part, layer, layers):
+        return pltpu.make_async_remote_copy(
+            state.at[B, pl.ds(layer, layers)], x0.at[B, pl.ds(layer + 1, layers)],
+            raw_send.at[part], raw_recv.at[part], {"tm": 0}, MESH)
+
+    raws = [raw(0, 0, 1), raw(1, depth - 1, 1), raw(2, 1, depth - 2)]
+    send_pick = pltpu.make_async_remote_copy(pick_out, pick, raw_send.at[3], raw_recv.at[3], {"tm": 0}, MESH)
 
     def step_into(src, dst, offset, snap, p, summed=False):
         for layer in (p, depth - 1 - p):
-            temper, dopant = layer_step(src, flow, snap, layer)
-            dst[0, layer + offset] = temper
-            dst[1, layer + offset] = dopant
+            flows = flow_at(flow, snap, layer)
+            temper = temper_step(src, flows, layer)
+            dst[A, layer + offset] = temper
+            dst[B, layer + offset] = dopant_step(src, flows, layer)
             if summed:
-                total[layer] = src[0, layer + 1] + temper
+                total[layer] = src[A, layer + 1] + temper
 
     @pl.when(first_phase)
     def _():
-        send_halo(halo0)
-        clear_ends(x0, x1)
-        load_state.wait()
-
+        send_halo(halo0[A])
+        send_halo(halo0[B])
+
+    load_snaps.wait()
+
+    @pl.when(t == source)
+    def _():
+        for i in range(steps):
+            pick_out[i] = jnp.full(pick_out.shape[1:], snaps[0, i].astype(jnp.float32))
+        send_pick.start()
+        for each in raws:
+            each.start()
+
+    clear_ends(x0, x1)
+    pl.when(first_phase)(lambda: load_state.wait())
     load_flow.wait()
 
-    @pl.when(first_phase)
-    def _():
+    @pl.when(t == 0)
+    def _():
+        raws[0].wait_recv()
+        raws[1].wait_recv()
+        send_halo(relay0)
+        send_pick.wait_recv()
+        raws[2].wait_recv()
+
         @pl.loop(0, pairs)
         def _(i):
             p = pairs - 1 - i
 
             @pl.when(p == 0)
             def _():
-                recv_halo(halo0)
-
-            step_into(x0, x1, 1, snaps[0, steps - 1], p)
-
-        send_halo(halo1)
+                recv_halo(relay0)
+
+            for layer in (p, depth - 1 - p):
+                x1[B, layer + 1] = dopant_step(x0, flow_picked(flow, pick[steps - 1], layer), layer)
+
+        send_halo(halo1[B])
 
         @pl.loop(0, pairs)
         def _(i):
@@ -151,21 +206,67 @@
 
             @pl.when(p == 0)
             def _():
-                recv_halo(halo1)
-
-            step_into(x1, x2, 0, snaps[0, 0], p, summed=True)
+                recv_halo(halo1[B])
+
+            for layer in (p, depth - 1 - p):
+                x2[B, layer] = dopant_step(x1, flow_picked(flow, pick[0], layer), layer)
+
+        send_halo(halo2[B])
+        for p in range(pairs):
+            pass_pair(B, p, mate)
+
+    @pl.when(first_phase)
+    def _():
+        @pl.loop(0, pairs)
+        def _(i):
+            p = pairs - 1 - i
+
+            @pl.when(p == 0)
+            def _():
+                recv_halo(halo0[A])
+                recv_halo(halo0[B])
+
+            step_into(x0, x1, 1, snaps[0, steps - 1], p)
+
+        send_halo(halo1[A])
+        pl.when(t != source)(lambda: send_halo(halo1[B]))
+
+        @pl.loop(0, pairs)
+        def _(i):
+            p = pairs - 1 - i
+
+            @pl.when(p == 0)
+            def _():
+                recv_halo(halo1[A])
+                pl.when(t != source)(lambda: recv_halo(halo1[B]))
+
+            for layer in (p, depth - 1 - p):
+                flows = flow_at(flow, snaps[0, 0], layer)
+                temper = temper_step(x1, flows, layer)
+                x2[A, layer] = temper
+                total[layer] = x1[A, layer + 1] + temper
+
+            @pl.when(t != source)
+            def _():
+                for layer in (p, depth - 1 - p):
+                    x2[B, layer] = dopant_step(x1, flow_at(flow, snaps[0, 0], layer), layer)
 
             @pl.when(p == pairs - 1)
             def _():
-                passing(p, t - 1).start()
-                passing(depth - 1 - p, t - 1).start()
-
-        send_halo(halo2)
+                pass_pair(A, p, t - 1)
+
+        send_halo(halo2[A])
+        pl.when(t != source)(lambda: send_halo(halo2[B]))
 
         @pl.loop(0, pairs - 1)
         def _(p):
-            passing(p, t - 1).start()
-            passing(depth - 1 - p, t - 1).start()
+            pass_pair(A, p, t - 1)
+
+        @pl.when(t != source)
+        def _():
+            @pl.loop(0, pairs)
+            def _(p):
+                pass_pair(B, p, mate)
 
     rows = total.shape[1] // slabs
     parts = ((1, depth - 2), (0, 1), (depth - 1, 1))
@@ -231,17 +332,17 @@
     def _():
         clear_ends(y0, y1)
 
-        def arrived(p):
-            passing(p, t + 1).wait_recv()
-            passing(depth - 1 - p, t + 1).wait_recv()
-
-        arrived(0)
-        slow = t == 1
+        slow = t == source - 1
+
+        for p in range(pairs):
+            arrived(B, p, mate)
+
+        arrived(A, 0, t + 1)
 
         @pl.when(jnp.logical_not(slow))
         def _():
             for p in range(1, pairs):
-                arrived(p)
+                arrived(A, p, t + 1)
 
         @pl.loop(0, pairs)
         def _(i):
@@ -249,17 +350,19 @@
 
             @pl.when(jnp.logical_and(slow, i < pairs - 1))
             def _():
-                arrived(i + 1)
-
-            @pl.when(p == 0)
-            def _():
-                recv_halo(halo2)
+                arrived(A, i + 1, t + 1)
+
+            @pl.when(p == 0)
+            def _():
+                recv_halo(halo2[A])
+                recv_halo(halo2[B])
 
             step_into(y0, y1, 1, snaps[0, steps - 1], p)
 
             @pl.when(p == 0)
             def _():
-                send_halo(halo3)
+                send_halo(halo3[A])
+                send_halo(halo3[B])
 
         @pl.loop(0, pairs)
         def _(i):
@@ -268,7 +371,8 @@
             @pl.when(p == 0)
             def _():
                 give(inner)
-                recv_halo(halo3)
+                recv_halo(halo3[A])
+                recv_halo(halo3[B])
 
             step_into(y1, y2, 0, snaps[0, 0], p, summed=True)
 
@@ -314,19 +418,38 @@
         grad[...] = (mine(3) + from_late[...] + from_early[...]) * scale
         mate3.wait_send()
 
+    @pl.when(t == 0)
+    def _():
+        sent_halo(relay0)
+
+    @pl.when(t == source)
+    def _():
+        send_pick.wait_send()
+        for each in raws:
+            each.wait_send()
+
     @pl.when(first_phase)
     def _():
-        sent_halo(halo0)
-        sent_halo(halo1)
-        sent_halo(halo2)
+        for each in (halo0[A], halo0[B], halo1[A], halo2[A]):
+            sent_halo(each)
 
         @pl.loop(0, depth)
         def _(layer):
-            passing(layer, t - 1).wait_send()
+            passing(A, layer, t - 1).wait_send()
+
+    @pl.when(t != source)
+    def _():
+        sent_halo(halo1[B])
+        sent_halo(halo2[B])
+
+        @pl.loop(0, depth)
+        def _(layer):
+            passing(B, layer, mate).wait_send()
 
     @pl.when(second_phase)
     def _():
-        sent_halo(halo3)
+        sent_halo(halo3[A])
+        sent_halo(halo3[B])
         store_mid.wait()
 
     pl.when(t == slabs - 1)(lambda: store_end.wait())
@@ -347,9 +470,9 @@
             jax.ShapeDtypeStruct((depth, rows, nz), f32),
         ),
         in_specs=[
-            pl.BlockSpec(memory_space=pl.ANY),
-            pl.BlockSpec(memory_space=pl.ANY),
-            pl.BlockSpec(memory_space=pltpu.SMEM),
+            pl.BlockSpec(memory_space=pltpu.HBM),
+            pl.BlockSpec(memory_space=pltpu.HBM),
+            pl.BlockSpec(memory_space=pltpu.HBM),
         ],
         out_specs=(pl.BlockSpec(memory_space=pl.ANY), pl.BlockSpec(memory_space=pltpu.VMEM)),
         scratch_shapes=[
@@ -359,10 +482,14 @@
             pltpu.VMEM((depth, 3 * rows, nz), f32),
             pltpu.VMEM((depth, rows, nz), f32),
             pltpu.VMEM((depth, rows, nz), f32),
-            dma((2,)), dma((4, 2)), dma((4, 2)), dma((depth,)), dma((depth,)), dma((slabs, 3)), dma((3, 3)), dma,
+            pltpu.SMEM(snap_of_step.shape, jnp.int32),
+            pltpu.VMEM((snap_of_step.shape[1], 8, 128), f32),
+            pltpu.VMEM((snap_of_step.shape[1], 8, 128), f32),
+            dma((3,)), dma((4, 2, 2)), dma((4, 2, 2)), dma((fields, depth)), dma((fields, depth)), dma((4,)), dma((4,)),
+            dma((slabs, 3)), dma((3, 3)), dma,
         ],
         compiler_params=pltpu.CompilerParams(
-            collective_id=0, has_side_effects=True, vmem_limit_bytes=60 * 1024 * 1024),
+            collective_id=0, has_side_effects=True, vmem_limit_bytes=32 * 1024 * 1024),
         cost_estimate=pl.CostEstimate(flops=200 * state.size, bytes_accessed=28 * state.size, transcendentals=0),
     )(state, velocity, snap_of_step)
     return final[None], gradient

time: 43.8 us -> 41.4 us (0.945)
  Pallas kernels: 38.8 us -> 35.1 us
  local copies, waits for them, and re-layouts: 3.86 us -> 5.39 us
    pallas_call x1, Pallas kernels: 38.8 us -> 35.1 us  [body(): pl.pallas_call(functools.partial(kernel, slabs, blocks), out_shape=(jax.S...]
    unnamed x2 -> x8, local copies, waits for them, and re-layouts: 3.86 us -> 5.39 us
where the time goes in v3:
time: 41.4 us; the launch traced here: 41.2 us
  Pallas kernels  35.1 us (85%)
  local copies, waits for them, and re-layouts  5.39 us (13%)
  between operations  0.65 us (2%)
    pallas_call x1, Pallas kernels, body(): pl.pallas_call(functools.partial(kernel, slabs, blocks), out_shape=(jax.S...  35.1 us
    unnamed x8, local copies, waits for them, and re-layouts  5.39 us

profile of v3, /device:TPU:21, one launch (start us, length us, event | category | flops | bytes accessed | tf_op | source)
XLA Modules:
  0.0 41.2 jit_solution(8013089661423637489)
XLA Ops:
  0.6 0.0 copy-start
  0.6 1.9 %copy-done = f32[2,3,8,32,512]{4,3,2,1,0:T(8,128)S(1)} copy-done((f32[2,3,8,32,512]{4,3,2,1,0:T(8,128)S(1)}, f32[2,3,8,32,512]{4,3,2,1,0:T(8,128)}, u32[]{:S(2)}) %copy-start) | copy-done | bytes 3145752
  2.5 0.0 copy-start.1
  2.5 1.2 %copy-done.1 = f32[1,2,8,32,512]{4,3,2,1,0:T(8,128)S(1)} copy-done((f32[1,2,8,32,512]{4,3,2,1,0:T(8,128)S(1)}, f32[1,2,8,32,512]{4,3,2,1,0:T(8,128)}, u32[]{:S(2)}) %copy-start.1) | copy-done | bytes 1048600
  3.7 0.0 copy-start.2
  3.7 0.7 %copy-done.2 = s32[1,2]{1,0:T(1,128)S(1)} copy-done((s32[1,2]{1,0:T(1,128)S(1)}, s32[1,2]{1,0:T(1,128)}, u32[]{:S(2)}) %copy-start.2) | copy-done | bytes 32
  4.4 35.1 %shard_map.50 = (f32[2,8,32,512]{3,2,1,0:T(8,128)S(1)}, f32[8,8,512]{2,1,0:T(8,128)S(1)}) custom-call(f32[2,8,32,512]{3,2,1,0:T(8,128)S(1)} %bitcast.2, f32[2,3,8,32,512]{4,3,2,1,0:T(8,128)S(1)} %copy-done, s32[1,2]{1,0:T(1,128)S(1)} %copy-done.2), custom_call_target="tpu_custom_call" | custom-call | flops 52428800 | bytes 7340032 | tf_op jit(solution)/shard_map/pallas_call | solution.py:466
  39.5 1.0 %copy.7 = f32[1,2,8,32,512]{4,3,2,1,0:T(8,128)} copy(f32[1,2,8,32,512]{4,3,2,1,0:T(8,128)S(1)} %bitcast.3) | data formatting | bytes 2097152
  40.5 0.7 %copy.8 = f32[8,8,512]{2,1,0:T(8,128)} copy(f32[8,8,512]{2,1,0:T(8,128)S(1)} %get-tuple-element.9) | data formatting | bytes 262144
Async XLA Ops:
  0.6 1.9 %copy-start = (f32[2,3,8,32,512]{4,3,2,1,0:T(8,128)S(1)}, f32[2,3,8,32,512]{4,3,2,1,0:T(8,128)}, u32[]{:S(2)}) copy-start(f32[2,3,8,32,512]{4,3,2,1,0:T(8,128)} %velocity.1) | copy-start | bytes 9437188
  2.5 1.2 %copy-start.1 = (f32[1,2,8,32,512]{4,3,2,1,0:T(8,128)S(1)}, f32[1,2,8,32,512]{4,3,2,1,0:T(8,128)}, u32[]{:S(2)}) copy-start(f32[1,2,8,32,512]{4,3,2,1,0:T(8,128)} %param.3) | copy-start | bytes 3145732
  3.7 0.7 %copy-start.2 = (s32[1,2]{1,0:T(1,128)S(1)}, s32[1,2]{1,0:T(1,128)}, u32[]{:S(2)}) copy-start(s32[1,2]{1,0:T(1,128)} %snaps_in.1) | copy-start | bytes 28

commit v4 on v3

--- a/solution.py
+++ b/solution.py
@@ -491,7 +491,7 @@
         compiler_params=pltpu.CompilerParams(
             collective_id=0, has_side_effects=True, vmem_limit_bytes=32 * 1024 * 1024),
         cost_estimate=pl.CostEstimate(flops=200 * state.size, bytes_accessed=28 * state.size, transcendentals=0),
-    )(state, velocity, snap_of_step)
+    )(*(pltpu.with_memory_space_constraint(x, pltpu.HBM) for x in (state, velocity, snap_of_step)))
     return final[None], gradient
 
 

time: 41.4 us -> 37.4 us (0.903)
  local copies, waits for them, and re-layouts: 5.39 us -> 1.63 us
    unnamed x8 -> x2, local copies, waits for them, and re-layouts: 5.39 us -> 1.63 us
where the time goes in v4:
time: 37.4 us; the launch traced here: 37.2 us
  Pallas kernels  34.9 us (93%)
  local copies, waits for them, and re-layouts  1.63 us (4%)
  between operations  0.64 us (2%)
    pallas_call x1, Pallas kernels, body(): pl.pallas_call(functools.partial(kernel, slabs, blocks), out_shape=(jax.S...  34.9 us
    unnamed x2, local copies, waits for them, and re-layouts  1.63 us

profile of v4, /device:TPU:21, one launch (start us, length us, event | category | flops | bytes accessed | tf_op | source)
XLA Modules:
  0.0 37.2 jit_solution(9969577320142998904)
XLA Ops:
  0.6 34.9 %shard_map.50 = (f32[2,8,32,512]{3,2,1,0:T(8,128)S(1)}, f32[8,8,512]{2,1,0:T(8,128)S(1)}) custom-call(f32[2,8,32,512]{3,2,1,0:T(8,128)} %bitcast.3, f32[2,3,8,32,512]{4,3,2,1,0:T(8,128)} %velocity.1, s32[1,2]{1,0:T(1,128)} %snaps_in.1), custom_call_target="tpu_custom_call" | custom-call | flops 52428800 | bytes 7340032 | tf_op jit(solution)/shard_map/pallas_call | solution.py:466
  35.6 1.0 %copy.7 = f32[1,2,8,32,512]{4,3,2,1,0:T(8,128)} copy(f32[1,2,8,32,512]{4,3,2,1,0:T(8,128)S(1)} %bitcast.2) | data formatting | bytes 2097152
  36.6 0.7 %copy.8 = f32[8,8,512]{2,1,0:T(8,128)} copy(f32[8,8,512]{2,1,0:T(8,128)S(1)} %get-tuple-element.9) | data formatting | bytes 262144

commit v5 on v4

--- a/solution.py
+++ b/solution.py
@@ -251,22 +251,15 @@
                 for layer in (p, depth - 1 - p):
                     x2[B, layer] = dopant_step(x1, flow_at(flow, snaps[0, 0], layer), layer)
 
-            @pl.when(p == pairs - 1)
+            @pl.when(p > 0)
             def _():
                 pass_pair(A, p, t - 1)
+                pl.when(t != source)(lambda: pass_pair(B, p, mate))
 
         send_halo(halo2[A])
         pl.when(t != source)(lambda: send_halo(halo2[B]))
-
-        @pl.loop(0, pairs - 1)
-        def _(p):
-            pass_pair(A, p, t - 1)
-
-        @pl.when(t != source)
-        def _():
-            @pl.loop(0, pairs)
-            def _(p):
-                pass_pair(B, p, mate)
+        pass_pair(A, 0, t - 1)
+        pl.when(t != source)(lambda: pass_pair(B, 0, mate))
 
     rows = total.shape[1] // slabs
     parts = ((1, depth - 2), (0, 1), (depth - 1, 1))
@@ -332,25 +325,16 @@
     def _():
         clear_ends(y0, y1)
 
-        slow = t == source - 1
-
-        for p in range(pairs):
+        def ready(p):
             arrived(B, p, mate)
-
-        arrived(A, 0, t + 1)
-
-        @pl.when(jnp.logical_not(slow))
-        def _():
-            for p in range(1, pairs):
-                arrived(A, p, t + 1)
+            arrived(A, p, t + 1)
+
+        ready(pairs - 1)
 
         @pl.loop(0, pairs)
         def _(i):
-            p = lax.rem(i + jnp.where(slow, 0, 1), pairs)
-
-            @pl.when(jnp.logical_and(slow, i < pairs - 1))
-            def _():
-                arrived(A, i + 1, t + 1)
+            p = jnp.where(i < pairs - 2, pairs - 1 - i, i - (pairs - 2))
+            pl.when(i < pairs - 1)(lambda: ready(pairs - 2 - i))
 
             @pl.when(p == 0)
             def _():
@@ -453,6 +437,24 @@
         store_mid.wait()
 
     pl.when(t == slabs - 1)(lambda: store_end.wait())
+
+
+def write_kernel(final, grad, final_out, grad_out, sems):
+    copies = [pltpu.make_async_copy(final, final_out, sems.at[0]), pltpu.make_async_copy(grad, grad_out, sems.at[1])]
+    for each in copies:
+        each.start()
+    for each in copies:
+        each.wait()
+
+
+def written(final, gradient):
+    return pl.pallas_call(
+        write_kernel,
+        out_shape=[jax.ShapeDtypeStruct(x.shape, x.dtype) for x in (final, gradient)],
+        in_specs=[pl.BlockSpec(memory_space=pl.ANY)] * 2,
+        out_specs=[pl.BlockSpec(memory_space=pl.ANY)] * 2,
+        scratch_shapes=[pltpu.SemaphoreType.DMA((2,))],
+    )(final, gradient)
 
 
 def body(slabs, blocks, slab_states, velocity, snap_of_step):
@@ -492,6 +494,7 @@
             collective_id=0, has_side_effects=True, vmem_limit_bytes=32 * 1024 * 1024),
         cost_estimate=pl.CostEstimate(flops=200 * state.size, bytes_accessed=28 * state.size, transcendentals=0),
     )(*(pltpu.with_memory_space_constraint(x, pltpu.HBM) for x in (state, velocity, snap_of_step)))
+    final, gradient = written(final, gradient)
     return final[None], gradient
 
 

time: 37.4 us -> 74.6 us (1.99)
  Pallas kernels: 34.9 us -> 72.2 us
    pallas_call x0 -> x1, Pallas kernels: none -> 36.9 us  [written(): pl.pallas_call(write_kernel, out_shape=[jax.ShapeDtypeStruct(x.shape, x.d...]
    unnamed x2 -> x4, local copies, waits for them, and re-layouts: 1.63 us -> 1.61 us
where the time goes in v5:
time: 74.6 us; the launch traced here: 74.4 us
  Pallas kernels  72.2 us (97%)
  local copies, waits for them, and re-layouts  1.61 us (2%)
    pallas_call x1, Pallas kernels, written(): pl.pallas_call(write_kernel, out_shape=[jax.ShapeDtypeStruct(x.shape, x.d...  36.9 us
    pallas_call x1, Pallas kernels, body(): pl.pallas_call(functools.partial(kernel, slabs, blocks), out_shape=(jax.S...  35.3 us
    unnamed x4, local copies, waits for them, and re-layouts  1.61 us

profile of v5, /device:TPU:21, one launch (start us, length us, event | category | flops | bytes accessed | tf_op | source)
XLA Modules:
  0.0 74.4 jit_solution(18094210889927089009)
XLA Ops:
  0.6 35.3 %shard_map.50 = (f32[2,8,32,512]{3,2,1,0:T(8,128)S(1)}, f32[8,8,512]{2,1,0:T(8,128)S(1)}) custom-call(f32[2,8,32,512]{3,2,1,0:T(8,128)} %bitcast.2, f32[2,3,8,32,512]{4,3,2,1,0:T(8,128)} %velocity.1, s32[1,2]{1,0:T(1,128)} %snaps_in.1), custom_call_target="tpu_custom_call" | custom-call | flops 52428800 | bytes 7340032 | tf_op jit(solution)/shard_map/pallas_call | solution.py:468
  36.0 0.0 copy-start
  36.0 1.0 %copy-done = f32[2,8,32,512]{3,2,1,0:T(8,128)} copy-done((f32[2,8,32,512]{3,2,1,0:T(8,128)}, f32[2,8,32,512]{3,2,1,0:T(8,128)S(1)}, u32[]{:S(2)}) %copy-start) | copy-done | bytes 1048600
  36.9 0.0 copy-start.1
  36.9 0.6 copy-done.1
  37.6 36.9 %shard_map.51 = (f32[2,8,32,512]{3,2,1,0:T(8,128)}, f32[8,8,512]{2,1,0:T(8,128)}) custom-call(f32[2,8,32,512]{3,2,1,0:T(8,128)} %copy-done, f32[8,8,512]{2,1,0:T(8,128)} %copy-done.1), custom_call_target="tpu_custom_call" | custom-call | tf_op jit(solution)/shard_map/pallas_call | solution.py:451
Async XLA Ops:
  36.0 1.0 %copy-start = (f32[2,8,32,512]{3,2,1,0:T(8,128)}, f32[2,8,32,512]{3,2,1,0:T(8,128)S(1)}, u32[]{:S(2)}) copy-start(f32[2,8,32,512]{3,2,1,0:T(8,128)S(1)} %get-tuple-element.6.final) | copy-start | bytes 3145732
  36.9 0.6 copy-start.1

commit v6 on v5

--- a/solution.py
+++ b/solution.py
@@ -13,12 +13,16 @@
 
 def shifted(field):
     rows, lanes = field.shape
-    row = lax.broadcasted_iota(jnp.int32, field.shape, 0)
-    lane = lax.broadcasted_iota(jnp.int32, field.shape, 1)
-    north = jnp.where(row == rows - 1, 0.0, pltpu.roll(field, rows - 1, 0))
-    south = jnp.where(row == 0, 0.0, pltpu.roll(field, 1, 0))
-    upper = jnp.where(lane == lanes - 1, 0.0, pltpu.roll(field, lanes - 1, 1))
-    lower = jnp.where(lane == 0, 0.0, pltpu.roll(field, 1, 1))
+    row = lax.broadcasted_iota(jnp.int32, (8, lanes), 0)
+    lane = lax.broadcasted_iota(jnp.int32, (rows, 128), 1)
+    north = pltpu.roll(field, rows - 1, 0)
+    north = jnp.concatenate([north[:-8], jnp.where(row == 7, 0.0, north[-8:])], axis=0)
+    south = pltpu.roll(field, 1, 0)
+    south = jnp.concatenate([jnp.where(row == 0, 0.0, south[:8]), south[8:]], axis=0)
+    upper = pltpu.roll(field, lanes - 1, 1)
+    upper = jnp.concatenate([upper[:, :-128], jnp.where(lane == 127, 0.0, upper[:, -128:])], axis=1)
+    lower = pltpu.roll(field, 1, 1)
+    lower = jnp.concatenate([jnp.where(lane == 0, 0.0, lower[:, :128]), lower[:, 128:]], axis=1)
     return north, south, upper, lower
 
 
@@ -262,8 +266,8 @@
         pl.when(t != source)(lambda: pass_pair(B, 0, mate))
 
     rows = total.shape[1] // slabs
-    parts = ((1, depth - 2), (0, 1), (depth - 1, 1))
-    inner, outer = (0,), (1, 2)
+    parts = ((2, depth - 4), (1, 1), (depth - 2, 1), (0, 1), (depth - 1, 1))
+    inner, second, outer = (0,), (1, 2), (3, 4)
 
     class Share:
         def __init__(self, first, count, dst, slot, target):
@@ -275,7 +279,7 @@
                 for part, (layer, layers) in enumerate(parts)
             ]
 
-        def start(self, which=inner + outer):
+        def start(self, which=inner + second + outer):
             for part in which:
                 self.copies[part].start()
 
@@ -354,11 +358,12 @@
 
             @pl.when(p == 0)
             def _():
-                give(inner)
                 recv_halo(halo3[A])
                 recv_halo(halo3[B])
 
             step_into(y1, y2, 0, snaps[0, 0], p, summed=True)
+            pl.when(p == 2)(lambda: give(inner))
+            pl.when(p == 1)(lambda: give(second))
 
         give(outer)
 
@@ -451,10 +456,10 @@
     return pl.pallas_call(
         write_kernel,
         out_shape=[jax.ShapeDtypeStruct(x.shape, x.dtype) for x in (final, gradient)],
-        in_specs=[pl.BlockSpec(memory_space=pl.ANY)] * 2,
+        in_specs=[pl.BlockSpec(memory_space=pltpu.VMEM)] * 2,
         out_specs=[pl.BlockSpec(memory_space=pl.ANY)] * 2,
         scratch_shapes=[pltpu.SemaphoreType.DMA((2,))],
-    )(final, gradient)
+    )(*(pltpu.with_memory_space_constraint(x, pltpu.VMEM) for x in (final, gradient)))
 
 
 def body(slabs, blocks, slab_states, velocity, snap_of_step):
@@ -488,7 +493,7 @@
             pltpu.VMEM((snap_of_step.shape[1], 8, 128), f32),
             pltpu.VMEM((snap_of_step.shape[1], 8, 128), f32),
             dma((3,)), dma((4, 2, 2)), dma((4, 2, 2)), dma((fields, depth)), dma((fields, depth)), dma((4,)), dma((4,)),
-            dma((slabs, 3)), dma((3, 3)), dma,
+            dma((slabs, 5)), dma((3, 5)), dma,
         ],
         compiler_params=pltpu.CompilerParams(
             collective_id=0, has_side_effects=True, vmem_limit_bytes=32 * 1024 * 1024),

time: 74.6 us -> 37.2 us (0.50)
  Pallas kernels: 72.2 us -> 36.5 us
  local copies, waits for them, and re-layouts: 1.61 us -> 0 us
    pallas_call x1, Pallas kernels: 36.9 us -> 1.02 us  [written(): pl.pallas_call(write_kernel, out_shape=[jax.ShapeDtypeStruct(x.shape, x.d...]
    unnamed x4 -> x0, local copies, waits for them, and re-layouts: 1.61 us -> none
where the time goes in v6:
time: 37.2 us; the launch traced here: 37.1 us
  Pallas kernels  36.5 us (98%)
  between operations  0.64 us (2%)
    pallas_call x1, Pallas kernels, body(): pl.pallas_call(functools.partial(kernel, slabs, blocks), out_shape=(jax.S...  35.4 us
    pallas_call x1, Pallas kernels, written(): pl.pallas_call(write_kernel, out_shape=[jax.ShapeDtypeStruct(x.shape, x.d...  1.02 us

profile of v6, /device:TPU:21, one launch (start us, length us, event | category | flops | bytes accessed | tf_op | source)
XLA Modules:
  0.0 37.1 jit_solution(8589421969560390110)
XLA Ops:
  0.6 35.4 %shard_map.50 = (f32[2,8,32,512]{3,2,1,0:T(8,128)S(1)}, f32[8,8,512]{2,1,0:T(8,128)S(1)}) custom-call(f32[2,8,32,512]{3,2,1,0:T(8,128)} %bitcast.2, f32[2,3,8,32,512]{4,3,2,1,0:T(8,128)} %velocity.1, s32[1,2]{1,0:T(1,128)} %snaps_in.1), custom_call_target="tpu_custom_call" | custom-call | flops 52428800 | bytes 7340032 | tf_op jit(solution)/shard_map/pallas_call | solution.py:473
  36.1 1.0 %shard_map.51 = (f32[2,8,32,512]{3,2,1,0:T(8,128)}, f32[8,8,512]{2,1,0:T(8,128)}) custom-call(f32[2,8,32,512]{3,2,1,0:T(8,128)S(1)} %get-tuple-element.6.final, f32[8,8,512]{2,1,0:T(8,128)S(1)} %get-tuple-element.7.grad), custom_call_target="tpu_custom_call" | custom-call | tf_op jit(solution)/shard_map/pallas_call | solution.py:456

commit v7 on v6

--- a/solution.py
+++ b/solution.py
@@ -129,7 +129,6 @@
 
     A, B = 0, 1
     halo0 = [halo(0, f, state.at[f, 0], state.at[f, depth - 1], x0) for f in (A, B)]
-    relay0 = halo(0, B, x0.at[B, 1], x0.at[B, depth], x0)
     halo1 = [halo(1, f, x1.at[f, 1], x1.at[f, depth], x1) for f in (A, B)]
     halo2 = [halo(2, f, x2.at[f, 0], x2.at[f, depth - 1], y0, (t - 1, mate)[f]) for f in (A, B)]
     halo3 = [halo(3, f, y1.at[f, 1], y1.at[f, depth], y1) for f in (A, B)]
@@ -147,12 +146,11 @@
         passing(field, p, origin).wait_recv()
         passing(field, depth - 1 - p, origin).wait_recv()
 
-    def raw(part, layer, layers):
-        return pltpu.make_async_remote_copy(
-            state.at[B, pl.ds(layer, layers)], x0.at[B, pl.ds(layer + 1, layers)],
-            raw_send.at[part], raw_recv.at[part], {"tm": 0}, MESH)
-
-    raws = [raw(0, 0, 1), raw(1, depth - 1, 1), raw(2, 1, depth - 2)]
+    def half(part, layer, layers):
+        there = x1.at[B, pl.ds(layer + 1, layers)]
+        return pltpu.make_async_remote_copy(there, there, raw_send.at[part], raw_recv.at[part], {"tm": 0}, MESH)
+
+    halves = [half(0, 0, 1), half(1, depth - 1, 1), half(2, 1, depth - 2)]
     send_pick = pltpu.make_async_remote_copy(pick_out, pick, raw_send.at[3], raw_recv.at[3], {"tm": 0}, MESH)
 
     def step_into(src, dst, offset, snap, p, summed=False):
@@ -164,20 +162,30 @@
             if summed:
                 total[layer] = src[A, layer + 1] + temper
 
+    ends = (0, depth - 1)
+
+    def end_dopant(src, dst, offset, snap):
+        for layer in ends:
+            dst[B, layer + offset] = dopant_step(src, flow_at(flow, snap, layer), layer)
+
+    def end_temper(src, dst, offset, snap, summed=False):
+        for layer in ends:
+            temper = temper_step(src, flow_at(flow, snap, layer), layer)
+            dst[A, layer + offset] = temper
+            if summed:
+                total[layer] = src[A, layer + 1] + temper
+
     @pl.when(first_phase)
     def _():
+        send_halo(halo0[B])
         send_halo(halo0[A])
-        send_halo(halo0[B])
 
     load_snaps.wait()
 
     @pl.when(t == source)
     def _():
-        for i in range(steps):
-            pick_out[i] = jnp.full(pick_out.shape[1:], snaps[0, i].astype(jnp.float32))
+        pick_out[...] = jnp.full(pick_out.shape, snaps[0, 0].astype(jnp.float32))
         send_pick.start()
-        for each in raws:
-            each.start()
 
     clear_ends(x0, x1)
     pl.when(first_phase)(lambda: load_state.wait())
@@ -185,85 +193,74 @@
 
     @pl.when(t == 0)
     def _():
-        raws[0].wait_recv()
-        raws[1].wait_recv()
-        send_halo(relay0)
+        def picked_step(layer):
+            x2[B, layer] = dopant_step(x1, flow_picked(flow, pick[...], layer), layer)
+
+        halves[0].wait_recv()
+        halves[1].wait_recv()
+        send_halo(halo1[B])
         send_pick.wait_recv()
-        raws[2].wait_recv()
-
-        @pl.loop(0, pairs)
-        def _(i):
-            p = pairs - 1 - i
-
-            @pl.when(p == 0)
-            def _():
-                recv_halo(relay0)
-
-            for layer in (p, depth - 1 - p):
-                x1[B, layer + 1] = dopant_step(x0, flow_picked(flow, pick[steps - 1], layer), layer)
-
-        send_halo(halo1[B])
-
-        @pl.loop(0, pairs)
-        def _(i):
-            p = pairs - 1 - i
-
-            @pl.when(p == 0)
-            def _():
-                recv_halo(halo1[B])
-
-            for layer in (p, depth - 1 - p):
-                x2[B, layer] = dopant_step(x1, flow_picked(flow, pick[0], layer), layer)
-
+        halves[2].wait_recv()
+
+        @pl.loop(1, depth - 1)
+        def _(layer):
+            picked_step(layer)
+
+        recv_halo(halo1[B])
+        for layer in ends:
+            picked_step(layer)
         send_halo(halo2[B])
         for p in range(pairs):
             pass_pair(B, p, mate)
 
     @pl.when(first_phase)
     def _():
-        @pl.loop(0, pairs)
+        snap = snaps[0, steps - 1]
+
+        @pl.loop(0, pairs - 1)
+        def _(i):
+            step_into(x0, x1, 1, snap, pairs - 1 - i)
+
+        recv_halo(halo0[B])
+        end_dopant(x0, x1, 1, snap)
+        pl.when(t != source)(lambda: send_halo(halo1[B]))
+
+        @pl.when(t == source)
+        def _():
+            for each in halves:
+                each.start()
+
+        recv_halo(halo0[A])
+        end_temper(x0, x1, 1, snap)
+        send_halo(halo1[A])
+        snap = snaps[0, 0]
+
+        @pl.loop(0, pairs - 1)
         def _(i):
             p = pairs - 1 - i
-
-            @pl.when(p == 0)
-            def _():
-                recv_halo(halo0[A])
-                recv_halo(halo0[B])
-
-            step_into(x0, x1, 1, snaps[0, steps - 1], p)
-
-        send_halo(halo1[A])
-        pl.when(t != source)(lambda: send_halo(halo1[B]))
-
-        @pl.loop(0, pairs)
-        def _(i):
-            p = pairs - 1 - i
-
-            @pl.when(p == 0)
-            def _():
-                recv_halo(halo1[A])
-                pl.when(t != source)(lambda: recv_halo(halo1[B]))
-
             for layer in (p, depth - 1 - p):
-                flows = flow_at(flow, snaps[0, 0], layer)
-                temper = temper_step(x1, flows, layer)
+                temper = temper_step(x1, flow_at(flow, snap, layer), layer)
                 x2[A, layer] = temper
                 total[layer] = x1[A, layer + 1] + temper
+            pass_pair(A, p, t - 1)
 
             @pl.when(t != source)
             def _():
                 for layer in (p, depth - 1 - p):
-                    x2[B, layer] = dopant_step(x1, flow_at(flow, snaps[0, 0], layer), layer)
-
-            @pl.when(p > 0)
-            def _():
-                pass_pair(A, p, t - 1)
-                pl.when(t != source)(lambda: pass_pair(B, p, mate))
-
+                    x2[B, layer] = dopant_step(x1, flow_at(flow, snap, layer), layer)
+                pass_pair(B, p, mate)
+
+        @pl.when(t != source)
+        def _():
+            recv_halo(halo1[B])
+            end_dopant(x1, x2, 0, snap)
+            send_halo(halo2[B])
+            pass_pair(B, 0, mate)
+
+        recv_halo(halo1[A])
+        end_temper(x1, x2, 0, snap, summed=True)
         send_halo(halo2[A])
-        pl.when(t != source)(lambda: send_halo(halo2[B]))
         pass_pair(A, 0, t - 1)
-        pl.when(t != source)(lambda: pass_pair(B, 0, mate))
 
     rows = total.shape[1] // slabs
     parts = ((2, depth - 4), (1, 1), (depth - 2, 1), (0, 1), (depth - 1, 1))
@@ -333,38 +330,36 @@
             arrived(B, p, mate)
             arrived(A, p, t + 1)
 
+        snap = snaps[0, steps - 1]
         ready(pairs - 1)
 
-        @pl.loop(0, pairs)
+        @pl.loop(0, pairs - 2)
         def _(i):
-            p = jnp.where(i < pairs - 2, pairs - 1 - i, i - (pairs - 2))
-            pl.when(i < pairs - 1)(lambda: ready(pairs - 2 - i))
-
-            @pl.when(p == 0)
-            def _():
-                recv_halo(halo2[A])
-                recv_halo(halo2[B])
-
-            step_into(y0, y1, 1, snaps[0, steps - 1], p)
-
-            @pl.when(p == 0)
-            def _():
-                send_halo(halo3[A])
-                send_halo(halo3[B])
-
-        @pl.loop(0, pairs)
+            ready(pairs - 2 - i)
+            step_into(y0, y1, 1, snap, pairs - 1 - i)
+
+        arrived(B, 0, mate)
+        recv_halo(halo2[B])
+        end_dopant(y0, y1, 1, snap)
+        send_halo(halo3[B])
+        arrived(A, 0, t + 1)
+        recv_halo(halo2[A])
+        end_temper(y0, y1, 1, snap)
+        send_halo(halo3[A])
+        step_into(y0, y1, 1, snap, 1)
+        snap = snaps[0, 0]
+
+        @pl.loop(0, pairs - 1)
         def _(i):
             p = pairs - 1 - i
-
-            @pl.when(p == 0)
-            def _():
-                recv_halo(halo3[A])
-                recv_halo(halo3[B])
-
-            step_into(y1, y2, 0, snaps[0, 0], p, summed=True)
+            step_into(y1, y2, 0, snap, p, summed=True)
             pl.when(p == 2)(lambda: give(inner))
             pl.when(p == 1)(lambda: give(second))
 
+        recv_halo(halo3[B])
+        end_dopant(y1, y2, 0, snap)
+        recv_halo(halo3[A])
+        end_temper(y1, y2, 0, snap, summed=True)
         give(outer)
 
     store_mid = pltpu.make_async_copy(y2, out, out_sem)
@@ -407,14 +402,10 @@
         grad[...] = (mine(3) + from_late[...] + from_early[...]) * scale
         mate3.wait_send()
 
-    @pl.when(t == 0)
-    def _():
-        sent_halo(relay0)
-
     @pl.when(t == source)
     def _():
         send_pick.wait_send()
-        for each in raws:
+        for each in halves:
             each.wait_send()
 
     @pl.when(first_phase)
@@ -490,8 +481,8 @@
             pltpu.VMEM((depth, rows, nz), f32),
             pltpu.VMEM((depth, rows, nz), f32),
             pltpu.SMEM(snap_of_step.shape, jnp.int32),
-            pltpu.VMEM((snap_of_step.shape[1], 8, 128), f32),
-            pltpu.VMEM((snap_of_step.shape[1], 8, 128), f32),
+            pltpu.VMEM((8, 128), f32),
+            pltpu.VMEM((8, 128), f32),
             dma((3,)), dma((4, 2, 2)), dma((4, 2, 2)), dma((fields, depth)), dma((fields, depth)), dma((4,)), dma((4,)),
             dma((slabs, 5)), dma((3, 5)), dma,
         ],

time: 37.2 us -> 33.9 us (0.911); the launches traced: 37.1 us -> 33.4 us
  Pallas kernels: 36.5 us -> 32.8 us
    pallas_call x1, Pallas kernels: 35.4 us -> 31.7 us  [body(): pl.pallas_call(functools.partial(kernel, slabs, blocks), out_shape=(jax.S...]
where the time goes in v7:
time: 33.9 us; the launch traced here: 33.4 us
  Pallas kernels  32.8 us (97%)
  between operations  0.64 us (2%)
    pallas_call x1, Pallas kernels, body(): pl.pallas_call(functools.partial(kernel, slabs, blocks), out_shape=(jax.S...  31.7 us
    pallas_call x1, Pallas kernels, written(): pl.pallas_call(write_kernel, out_shape=[jax.ShapeDtypeStruct(x.shape, x.d...  1.02 us

profile of v7, /device:TPU:21, one launch (start us, length us, event | category | flops | bytes accessed | tf_op | source)
XLA Modules:
  0.0 33.4 jit_solution(1512392261151881676)
XLA Ops:
  0.6 31.7 %shard_map.50 = (f32[2,8,32,512]{3,2,1,0:T(8,128)S(1)}, f32[8,8,512]{2,1,0:T(8,128)S(1)}) custom-call(f32[2,8,32,512]{3,2,1,0:T(8,128)} %bitcast.2, f32[2,3,8,32,512]{4,3,2,1,0:T(8,128)} %velocity.1, s32[1,2]{1,0:T(1,128)} %snaps_in.1), custom_call_target="tpu_custom_call" | custom-call | flops 52428800 | bytes 7340032 | tf_op jit(solution)/shard_map/pallas_call | solution.py:464
  32.4 1.0 %shard_map.51 = (f32[2,8,32,512]{3,2,1,0:T(8,128)}, f32[8,8,512]{2,1,0:T(8,128)}) custom-call(f32[2,8,32,512]{3,2,1,0:T(8,128)S(1)} %get-tuple-element.6.final, f32[8,8,512]{2,1,0:T(8,128)S(1)} %get-tuple-element.7.grad), custom_call_target="tpu_custom_call" | custom-call | tf_op jit(solution)/shard_map/pallas_call | solution.py:447

commit v8 on v7

--- a/solution.py
+++ b/solution.py
@@ -221,13 +221,14 @@
         def _(i):
             step_into(x0, x1, 1, snap, pairs - 1 - i)
 
+        pl.when(t == source)(lambda: halves[2].start())
         recv_halo(halo0[B])
         end_dopant(x0, x1, 1, snap)
         pl.when(t != source)(lambda: send_halo(halo1[B]))
 
         @pl.when(t == source)
         def _():
-            for each in halves:
+            for each in halves[:2]:
                 each.start()
 
         recv_halo(halo0[A])
@@ -331,13 +332,7 @@
             arrived(A, p, t + 1)
 
         snap = snaps[0, steps - 1]
-        ready(pairs - 1)
-
-        @pl.loop(0, pairs - 2)
-        def _(i):
-            ready(pairs - 2 - i)
-            step_into(y0, y1, 1, snap, pairs - 1 - i)
-
+        ready(1)
         arrived(B, 0, mate)
         recv_halo(halo2[B])
         end_dopant(y0, y1, 1, snap)
@@ -346,7 +341,14 @@
         recv_halo(halo2[A])
         end_temper(y0, y1, 1, snap)
         send_halo(halo3[A])
-        step_into(y0, y1, 1, snap, 1)
+
+        for p in range(2, pairs):
+            ready(p)
+
+        @pl.loop(0, pairs - 1)
+        def _(i):
+            step_into(y0, y1, 1, snap, pairs - 1 - i)
+
         snap = snaps[0, 0]
 
         @pl.loop(0, pairs - 1)

time: 33.9 us -> 36.3 us (1.071)
  Pallas kernels: 32.8 us -> 35.2 us
    pallas_call x1, Pallas kernels: 31.7 us -> 34.2 us  [body(): pl.pallas_call(functools.partial(kernel, slabs, blocks), out_shape=(jax.S...]
where the time goes in v8:
time: 36.3 us; the launch traced here: 35.8 us
  Pallas kernels  35.2 us (97%)
  between operations  0.64 us (2%)
    pallas_call x1, Pallas kernels, body(): pl.pallas_call(functools.partial(kernel, slabs, blocks), out_shape=(jax.S...  34.2 us
    pallas_call x1, Pallas kernels, written(): pl.pallas_call(write_kernel, out_shape=[jax.ShapeDtypeStruct(x.shape, x.d...  1.02 us

profile of v8, /device:TPU:21, one launch (start us, length us, event | category | flops | bytes accessed | tf_op | source)
XLA Modules:
  0.0 35.8 jit_solution(11988168890285833197)
XLA Ops:
  0.6 34.2 %shard_map.50 = (f32[2,8,32,512]{3,2,1,0:T(8,128)S(1)}, f32[8,8,512]{2,1,0:T(8,128)S(1)}) custom-call(f32[2,8,32,512]{3,2,1,0:T(8,128)} %bitcast.2, f32[2,3,8,32,512]{4,3,2,1,0:T(8,128)} %velocity.1, s32[1,2]{1,0:T(1,128)} %snaps_in.1), custom_call_target="tpu_custom_call" | custom-call | flops 52428800 | bytes 7340032 | tf_op jit(solution)/shard_map/pallas_call | solution.py:466
  34.8 1.0 %shard_map.51 = (f32[2,8,32,512]{3,2,1,0:T(8,128)}, f32[8,8,512]{2,1,0:T(8,128)}) custom-call(f32[2,8,32,512]{3,2,1,0:T(8,128)S(1)} %get-tuple-element.6.final, f32[8,8,512]{2,1,0:T(8,128)S(1)} %get-tuple-element.7.grad), custom_call_target="tpu_custom_call" | custom-call | tf_op jit(solution)/shard_map/pallas_call | solution.py:449

commit v9 on v8

--- a/solution.py
+++ b/solution.py
@@ -221,14 +221,13 @@
         def _(i):
             step_into(x0, x1, 1, snap, pairs - 1 - i)
 
-        pl.when(t == source)(lambda: halves[2].start())
         recv_halo(halo0[B])
         end_dopant(x0, x1, 1, snap)
         pl.when(t != source)(lambda: send_halo(halo1[B]))
 
         @pl.when(t == source)
         def _():
-            for each in halves[:2]:
+            for each in halves:
                 each.start()
 
         recv_halo(halo0[A])

time: 36.3 us -> 34.3 us (0.945)
  the two profiles are of different devices: /device:TPU:21 before, /device:TPU:13 now
where the time goes in v9:
time: 34.3 us; the launch traced here: 34.1 us
  Pallas kernels  33.5 us (98%)
  between operations  0.64 us (2%)
    pallas_call x1, Pallas kernels, body(): pl.pallas_call(functools.partial(kernel, slabs, blocks), out_shape=(jax.S...  32.5 us
    pallas_call x1, Pallas kernels, written(): pl.pallas_call(write_kernel, out_shape=[jax.ShapeDtypeStruct(x.shape, x.d...  1.02 us

profile of v9, /device:TPU:13, one launch (start us, length us, event | category | flops | bytes accessed | tf_op | source)
XLA Modules:
  0.0 34.1 jit_solution(14918829553505696668)
XLA Ops:
  0.6 32.5 %shard_map.50 = (f32[2,8,32,512]{3,2,1,0:T(8,128)S(1)}, f32[8,8,512]{2,1,0:T(8,128)S(1)}) custom-call(f32[2,8,32,512]{3,2,1,0:T(8,128)} %bitcast.2, f32[2,3,8,32,512]{4,3,2,1,0:T(8,128)} %velocity.1, s32[1,2]{1,0:T(1,128)} %snaps_in.1), custom_call_target="tpu_custom_call" | custom-call | flops 52428800 | bytes 7340032 | tf_op jit(solution)/shard_map/pallas_call | solution.py:465
  33.1 1.0 %shard_map.51 = (f32[2,8,32,512]{3,2,1,0:T(8,128)}, f32[8,8,512]{2,1,0:T(8,128)}) custom-call(f32[2,8,32,512]{3,2,1,0:T(8,128)S(1)} %get-tuple-element.6.final, f32[8,8,512]{2,1,0:T(8,128)S(1)} %get-tuple-element.7.grad), custom_call_target="tpu_custom_call" | custom-call | tf_op jit(solution)/shard_map/pallas_call | solution.py:448
